TPU v7x, 32 devices: a whole 2x2x4 slice. The times are simulated.
32 devices in a mesh: dp: 16 (over z, x, core), tensor: 2 (over y).
Axes of the slice: x: 2, y: 2, z: 4, core: 2. Of those that a mesh axis runs over, the one named last changes fastest.
Arguments:
- tokens: bfloat16 [8192, 1024], P(('dp', 'tensor')), may hold values from -6 to 6
- gain_attn: float32 [1024], replicated, may hold values from 0.5 to 1.5
- gain_ffn: float32 [1024], replicated, may hold values from 0.5 to 1.5
- w_query: bfloat16 [1024, 1024], P('dp', 'tensor'), may hold values from -0.1875 to 0.1875
- w_key: bfloat16 [1024, 512], P('dp', 'tensor'), may hold values from -0.1875 to 0.1875
- w_value: bfloat16 [1024, 512], P('dp', 'tensor'), may hold values from -0.1875 to 0.1875
- w_out: bfloat16 [1024, 1024], P('tensor', 'dp'), may hold values from -0.75 to 0.75
- w_gate: bfloat16 [32, 1024, 512], P('tensor', 'dp'), may hold values from -0.1875 to 0.1875
- w_up: bfloat16 [32, 1024, 512], P('tensor', 'dp'), may hold values from -0.1875 to 0.1875
- w_down: bfloat16 [32, 512, 1024], P('tensor', None, 'dp'), may hold values from -1 to 1
- route_gates: float32 [8192, 8], P('dp'), may hold values from 0 to 1, as said below
- routes: int32 [8192, 8], P('dp'), may hold values from 0 to 31, all different within a row; in each aligned block of 512 rows (0 to 511, 512 to 1023, ...) at most 160 rows name the same one
- cotangent: bfloat16 [8192, 1024], P(('dp', 'tensor')), may hold values from -6 to 6
Outputs:
- layer_out: bfloat16 [8192, 1024], P(('dp', 'tensor'))
- grad_tokens: float32 [8192, 1024], P(('dp', 'tensor'))
- grad_gates: float32 [8192, 8], P(('dp', 'tensor'))
- grad_gain_attn: float32 [1024], replicated
- grad_gain_ffn: float32 [1024], replicated
- grad_query: float32 [1024, 1024], P('dp', 'tensor')
- grad_key: float32 [1024, 512], P('dp', 'tensor')
- grad_value: float32 [1024, 512], P('dp', 'tensor')
- grad_out: float32 [1024, 1024], P('tensor', 'dp')
- grad_gate: float32 [32, 1024, 512], P('tensor', 'dp')
- grad_up: float32 [32, 1024, 512], P('tensor', 'dp')
- grad_down: float32 [32, 512, 1024], P('tensor', None, 'dp')
Inputs may be any that keep to these rules, and one draw needn't show every extreme that they name: `routes`: each row names 8 different experts; among the 512 rows of one index of dp no expert is named by more than 160 rows, a bound that some block reaches. `route_gates`: each row is positive and sums to one.
All inputs are finite; a program needn't handle non-finite values.
Results may differ from a plain program's by a relative error of at most 0.019.
Values may be sent and summed in bfloat16 or wider, within the bound.
A program may use at most 192 MiB of HBM per device.

v0:
```python
import jax
import jax.numpy as jnp
from jax import lax
from jax.sharding import PartitionSpec as P

D = 1024
HEAD_DIM = 64
EXPERTS = 32
TOP = 8
LEN = 1024


epsilon = 1e-06
rope_base = 10000.0
negative = -1e30


def rope_tables(count_rows, seq_length):
    positions = (jnp.arange(count_rows, dtype=jnp.int32) % seq_length).astype(jnp.float32)
    freqs = rope_base ** (
        -(jnp.arange(HEAD_DIM // 2, dtype=jnp.int32).astype(jnp.float32) * 2.0 / HEAD_DIM)
    )
    angles = positions[:, None] * freqs[None, :]
    return (
        jnp.concatenate([jnp.cos(angles), jnp.cos(angles)], -1),
        jnp.concatenate([jnp.sin(angles), jnp.sin(angles)], -1),
    )


def rotate(values, cosine, sine_table):
    halfway = values.shape[-1] // 2
    turned = jnp.concatenate([-values[..., halfway:], values[..., :halfway]], -1)
    return values * cosine[:, None, :] + turned * sine_table[:, None, :]


def rotate_back(grads, cosine, sine_table):
    halfway = grads.shape[-1] // 2
    shifted = grads * sine_table[:, None, :]
    reverted = jnp.concatenate([shifted[..., halfway:], -shifted[..., :halfway]], -1)
    return grads * cosine[:, None, :] + reverted


def normalize(values, gain_vector):
    factor = lax.rsqrt(jnp.mean(values * values, -1, keepdims=True) + epsilon)
    scaled = values * factor
    return ((scaled * gain_vector).astype(jnp.bfloat16), scaled, factor)


def normalize_back(grad_normed, scaled, factor, gain_vector):
    grad_scaled = grad_normed * gain_vector
    gain_term = jnp.sum(grad_normed * scaled, 0)
    grad_values = factor * (
        grad_scaled - scaled * jnp.mean(grad_scaled * scaled, -1, keepdims=True)
    )
    return (gain_term, grad_values)


def spread(values):
    return lax.all_gather(values, "tensor", axis=0, tiled=True)


def sum_rows(term, own_rows):
    return lax.psum_scatter(
        term(jnp.int32(0), lax.axis_size("tensor") * own_rows),
        "tensor",
        scatter_dimension=0,
        tiled=True,
    )


def dispatch(route_rows, first_expert, expert_count, capacity):
    flat_routes = route_rows.reshape(-1)
    offset_ids = flat_routes - first_expert
    onehot = (offset_ids[:, None] == jnp.arange(expert_count, dtype=jnp.int32)[None, :]).astype(
        jnp.int32
    )
    earlier = jnp.cumsum(onehot, 0) - onehot
    slot_index = jnp.sum(earlier * onehot, 1)
    owned = (offset_ids >= 0) & (offset_ids < expert_count)
    position = jnp.where(owned, offset_ids * capacity + slot_index, expert_count * capacity)
    numbers = jnp.arange(flat_routes.shape[0], dtype=jnp.int32) + 1
    slot_table = (
        jnp.zeros((expert_count * capacity + 1,), jnp.int32)
        .at[position]
        .set(numbers)[: expert_count * capacity]
    )
    filled = slot_table > 0
    source = jnp.maximum(slot_table - 1, 0)
    return (source // TOP, filled, source)


def block_scores(block_queries, seq_keys, start_row, block_rows, seq_length):
    raw_scores = jnp.einsum(
        "qgrd,kgd->grqk", block_queries, seq_keys, preferred_element_type=jnp.float32
    )
    query_pos = start_row + jnp.arange(block_rows, dtype=jnp.int32)[:, None]
    key_pos = jnp.arange(seq_length, dtype=jnp.int32)[None, :]
    return jnp.where(key_pos <= query_pos, raw_scores * HEAD_DIM ** (-0.5), negative)


def attend_forward(queries, key_rows, value_rows, seq_length, block_rows):
    row_count = queries.shape[0]
    kv_local = key_rows.shape[1]
    repeat_count = queries.shape[1] // kv_local
    seq_count = row_count // seq_length

    def one_sequence(pieces):
        seq_queries, seq_keys, seq_values = pieces
        out_blocks = []
        lse_blocks = []
        for block_index in range(seq_length // block_rows):
            start_row = block_index * block_rows
            block_queries = seq_queries[start_row : start_row + block_rows]
            scores = block_scores(block_queries, seq_keys, start_row, block_rows, seq_length)
            largest = jnp.max(scores, -1, keepdims=True)
            log_total = largest + jnp.log(jnp.sum(jnp.exp(scores - largest), -1, keepdims=True))
            probabilities = jnp.exp(scores - log_total).astype(jnp.bfloat16)
            block_out = jnp.einsum(
                "grqk,kgd->qgrd", probabilities, seq_values, preferred_element_type=jnp.float32
            )
            out_blocks.append(block_out.reshape(block_rows, -1))
            lse_blocks.append(log_total)
        return (jnp.concatenate(out_blocks, 0), jnp.concatenate(lse_blocks, 2))

    attended_values, log_sums = lax.map(
        one_sequence,
        (
            queries.reshape(seq_count, seq_length, kv_local, repeat_count, HEAD_DIM),
            key_rows.reshape(seq_count, seq_length, kv_local, HEAD_DIM),
            value_rows.reshape(seq_count, seq_length, kv_local, HEAD_DIM),
        ),
    )
    return (attended_values.reshape(row_count, -1), log_sums)


def attend_backward(queries, key_rows, value_rows, grad_mixed, log_sums, seq_length, block_rows):
    row_count = queries.shape[0]
    kv_local = key_rows.shape[1]
    repeat_count = queries.shape[1] // kv_local
    seq_count = row_count // seq_length
    scale = HEAD_DIM ** (-0.5)

    def one_sequence(pieces):
        seq_queries, seq_keys, seq_values, seq_grads, seq_sums = pieces
        grad_keys = jnp.zeros((seq_length, kv_local, HEAD_DIM), jnp.float32)
        grad_values = jnp.zeros((seq_length, kv_local, HEAD_DIM), jnp.float32)
        query_blocks = []
        for block_index in range(seq_length // block_rows):
            start_row = block_index * block_rows
            block_queries = seq_queries[start_row : start_row + block_rows]
            block_grads = seq_grads[start_row : start_row + block_rows]
            block_sums = seq_sums[:, :, start_row : start_row + block_rows]
            scores = block_scores(block_queries, seq_keys, start_row, block_rows, seq_length)
            probabilities = jnp.exp(scores - block_sums)
            rounded = probabilities.astype(jnp.bfloat16)
            grad_probs = jnp.einsum(
                "qgrd,kgd->grqk", block_grads, seq_values, preferred_element_type=jnp.float32
            )
            inner = jnp.sum(probabilities * grad_probs, -1, keepdims=True)
            grad_scores = (scale * probabilities * (grad_probs - inner)).astype(jnp.bfloat16)
            query_blocks.append(
                jnp.einsum(
                    "grqk,kgd->qgrd", grad_scores, seq_keys, preferred_element_type=jnp.float32
                )
            )
            grad_keys = grad_keys + jnp.einsum(
                "grqk,qgrd->kgd", grad_scores, block_queries, preferred_element_type=jnp.float32
            )
            grad_values = grad_values + jnp.einsum(
                "grqk,qgrd->kgd", rounded, block_grads, preferred_element_type=jnp.float32
            )
        return (jnp.concatenate(query_blocks, 0), grad_keys, grad_values)

    grad_queries, grad_keys, grad_values = lax.map(
        one_sequence,
        (
            queries.reshape(seq_count, seq_length, kv_local, repeat_count, HEAD_DIM),
            key_rows.reshape(seq_count, seq_length, kv_local, HEAD_DIM),
            value_rows.reshape(seq_count, seq_length, kv_local, HEAD_DIM),
            grad_mixed.reshape(seq_count, seq_length, kv_local, repeat_count, HEAD_DIM),
            log_sums,
        ),
    )
    return (
        grad_queries.reshape(row_count, kv_local * repeat_count, HEAD_DIM),
        grad_keys.reshape(row_count, kv_local, HEAD_DIM),
        grad_values.reshape(row_count, kv_local * HEAD_DIM),
    )


def on_device(
    tokens,
    gain_attn,
    gain_ffn,
    w_query,
    w_key,
    w_value,
    w_out,
    w_gate,
    w_up,
    w_down,
    route_gates,
    routes,
    cotangent,
):
    tensor_size = lax.axis_size("tensor")
    own_rows = tokens.shape[0]
    group_rows = own_rows * tensor_size
    seq_length = min(LEN, group_rows)
    block_rows = min(512, seq_length)
    capacity = group_rows * TOP * 5 // (4 * EXPERTS)
    local_experts = w_gate.shape[0]
    head_count = w_query.shape[1] // HEAD_DIM
    kv_count = w_key.shape[1] // HEAD_DIM
    cosine, sine_table = rope_tables(group_rows, seq_length)
    query_full, key_full, value_full, out_full = (
        lax.all_gather(w_query, "dp", axis=0, tiled=True),
        lax.all_gather(w_key, "dp", axis=0, tiled=True),
        lax.all_gather(w_value, "dp", axis=0, tiled=True),
        lax.all_gather(w_out, "dp", axis=1, tiled=True),
    )
    token_values = tokens.astype(jnp.float32)
    normed_own, scaled_attn, factor_attn = normalize(token_values, gain_attn)
    normed = spread(normed_own)
    query_pre = jnp.dot(normed, query_full, preferred_element_type=jnp.float32)
    key_pre = jnp.dot(normed, key_full, preferred_element_type=jnp.float32)
    value_pre = jnp.dot(normed, value_full, preferred_element_type=jnp.float32)
    queries = rotate(
        query_pre.reshape(group_rows, head_count, HEAD_DIM), cosine, sine_table
    ).astype(jnp.bfloat16)
    key_rows = rotate(key_pre.reshape(group_rows, kv_count, HEAD_DIM), cosine, sine_table).astype(
        jnp.bfloat16
    )
    value_rows = value_pre.reshape(group_rows, kv_count, HEAD_DIM).astype(jnp.bfloat16)
    attended_values, log_sums = attend_forward(
        queries, key_rows, value_rows, seq_length, block_rows
    )
    mixed = attended_values.astype(jnp.bfloat16)

    def out_term(start_row, row_span):
        return jnp.dot(
            lax.dynamic_slice_in_dim(mixed, start_row, row_span, 0),
            out_full,
            preferred_element_type=jnp.float32,
        )

    attended = token_values + sum_rows(out_term, own_rows)
    routed_own, scaled_ffn, factor_ffn = normalize(attended, gain_ffn)
    routed = spread(routed_own)
    gate_full, up_full, down_full = (
        lax.all_gather(w_gate, "dp", axis=1, tiled=True),
        lax.all_gather(w_up, "dp", axis=1, tiled=True),
        lax.all_gather(w_down, "dp", axis=2, tiled=True),
    )
    token_index, filled, source = dispatch(
        routes, lax.axis_index("tensor") * local_experts, local_experts, capacity
    )
    filled_rows = filled.astype(jnp.float32)
    slot_gate = route_gates.reshape(-1)[source] * filled_rows
    expert_in = (routed[token_index] * filled.astype(jnp.bfloat16)[:, None]).reshape(
        local_experts, capacity, D
    )
    gate_pre = jnp.einsum("ecd,edf->ecf", expert_in, gate_full, preferred_element_type=jnp.float32)
    up_pre = jnp.einsum("ecd,edf->ecf", expert_in, up_full, preferred_element_type=jnp.float32)
    sigmoid_gate = jax.nn.sigmoid(gate_pre)
    silu_gate = gate_pre * sigmoid_gate
    hidden = (silu_gate * up_pre).astype(jnp.bfloat16)
    expert_out = jnp.einsum(
        "ecf,efd->ecd", hidden, down_full, preferred_element_type=jnp.float32
    ).reshape(-1, D)
    combined = (
        jnp.zeros((group_rows, D), jnp.float32).at[token_index].add(slot_gate[:, None] * expert_out)
    )
    layer_out = (
        attended
        + lax.psum_scatter(
            combined.astype(jnp.bfloat16), "tensor", scatter_dimension=0, tiled=True
        ).astype(jnp.float32)
    ).astype(jnp.bfloat16)
    grad_full = spread(cotangent)
    gate_full, up_full, down_full = (
        lax.all_gather(w_gate, "dp", axis=1, tiled=True),
        lax.all_gather(w_up, "dp", axis=1, tiled=True),
        lax.all_gather(w_down, "dp", axis=2, tiled=True),
    )
    grad_slots = grad_full[token_index].astype(jnp.float32)
    gate_grad = jnp.sum(grad_slots * expert_out, -1) * filled_rows
    grad_expert = (
        (slot_gate[:, None] * grad_slots).astype(jnp.bfloat16).reshape(local_experts, capacity, D)
    )
    grad_down_w = jnp.einsum(
        "ecf,ecd->efd", hidden, grad_expert, preferred_element_type=jnp.float32
    )
    grad_hidden = jnp.einsum(
        "ecd,efd->ecf", grad_expert, down_full, preferred_element_type=jnp.float32
    )
    grad_gate_pre = (
        grad_hidden * up_pre * sigmoid_gate * (1.0 + gate_pre * (1.0 - sigmoid_gate))
    ).astype(jnp.bfloat16)
    grad_up_pre = (grad_hidden * silu_gate).astype(jnp.bfloat16)
    grad_gate_w = jnp.einsum(
        "ecd,ecf->edf", expert_in, grad_gate_pre, preferred_element_type=jnp.float32
    )
    grad_up_w = jnp.einsum(
        "ecd,ecf->edf", expert_in, grad_up_pre, preferred_element_type=jnp.float32
    )
    grad_expert_in = jnp.einsum(
        "ecf,edf->ecd", grad_gate_pre, gate_full, preferred_element_type=jnp.float32
    )
    grad_expert_in = grad_expert_in + jnp.einsum(
        "ecf,edf->ecd", grad_up_pre, up_full, preferred_element_type=jnp.float32
    )
    routed_part = (
        jnp.zeros((group_rows, D), jnp.float32)
        .at[token_index]
        .add(grad_expert_in.reshape(-1, D) * filled_rows[:, None])
    )
    gate_slots = jnp.where(filled, source, group_rows * TOP)
    gate_part = (
        jnp.zeros((group_rows * TOP + 1,), jnp.float32)
        .at[gate_slots]
        .add(gate_grad)[: group_rows * TOP]
        .reshape(group_rows, TOP)
    )
    grad_routed, grad_gates = (
        lax.psum_scatter(routed_part, "tensor", scatter_dimension=0, tiled=True),
        lax.psum_scatter(gate_part, "tensor", scatter_dimension=0, tiled=True),
    )
    gain_ffn_part, attended_norm = normalize_back(grad_routed, scaled_ffn, factor_ffn, gain_ffn)
    grad_attended = cotangent.astype(jnp.float32) + attended_norm
    grad_branch = spread(grad_attended.astype(jnp.bfloat16))
    query_full, key_full, value_full, out_full = (
        lax.all_gather(w_query, "dp", axis=0, tiled=True),
        lax.all_gather(w_key, "dp", axis=0, tiled=True),
        lax.all_gather(w_value, "dp", axis=0, tiled=True),
        lax.all_gather(w_out, "dp", axis=1, tiled=True),
    )
    grad_out_w = jnp.einsum("tc,td->cd", mixed, grad_branch, preferred_element_type=jnp.float32)
    grad_mixed = jnp.einsum(
        "td,cd->tc", grad_branch, out_full, preferred_element_type=jnp.float32
    ).astype(jnp.bfloat16)
    grad_queries, grad_keys, grad_values = attend_backward(
        queries, key_rows, value_rows, grad_mixed, log_sums, seq_length, block_rows
    )
    grad_query_pre = (
        rotate_back(grad_queries, cosine, sine_table).astype(jnp.bfloat16).reshape(group_rows, -1)
    )
    grad_key_pre = (
        rotate_back(grad_keys, cosine, sine_table).astype(jnp.bfloat16).reshape(group_rows, -1)
    )
    grad_value_pre = grad_values.astype(jnp.bfloat16)
    grad_query_w = jnp.einsum(
        "td,tc->dc", normed, grad_query_pre, preferred_element_type=jnp.float32
    )
    grad_key_w = jnp.einsum("td,tc->dc", normed, grad_key_pre, preferred_element_type=jnp.float32)
    grad_value_w = jnp.einsum(
        "td,tc->dc", normed, grad_value_pre, preferred_element_type=jnp.float32
    )

    def input_term(start_row, row_span):
        value_piece = lax.dynamic_slice_in_dim(grad_value_pre, start_row, row_span, 0)
        partial_sum = jnp.einsum(
            "tc,dc->td", grad_query_pre, query_full, preferred_element_type=jnp.float32
        )
        partial_sum = partial_sum + jnp.einsum(
            "tc,dc->td", grad_key_pre, key_full, preferred_element_type=jnp.float32
        )
        return partial_sum + jnp.einsum(
            "tc,dc->td", value_piece, value_full, preferred_element_type=jnp.float32
        )

    grad_normed = sum_rows(input_term, own_rows)
    gain_attn_part, tokens_norm = normalize_back(grad_normed, scaled_attn, factor_attn, gain_attn)
    grad_tokens = grad_attended + tokens_norm
    grad_gain_attn, grad_gain_ffn = lax.psum((gain_attn_part, gain_ffn_part), ("dp", "tensor"))
    grad_query, grad_key, grad_value, grad_out = (
        lax.psum_scatter(
            grad_query_w.astype(jnp.bfloat16), "dp", scatter_dimension=0, tiled=True
        ).astype(jnp.float32),
        lax.psum_scatter(
            grad_key_w.astype(jnp.bfloat16), "dp", scatter_dimension=0, tiled=True
        ).astype(jnp.float32),
        lax.psum_scatter(
            grad_value_w.astype(jnp.bfloat16), "dp", scatter_dimension=0, tiled=True
        ).astype(jnp.float32),
        lax.psum_scatter(
            grad_out_w.astype(jnp.bfloat16), "dp", scatter_dimension=1, tiled=True
        ).astype(jnp.float32),
    )
    grad_gate, grad_up, grad_down = (
        lax.psum_scatter(
            grad_gate_w.astype(jnp.bfloat16), "dp", scatter_dimension=1, tiled=True
        ).astype(jnp.float32),
        lax.psum_scatter(
            grad_up_w.astype(jnp.bfloat16), "dp", scatter_dimension=1, tiled=True
        ).astype(jnp.float32),
        lax.psum_scatter(
            grad_down_w.astype(jnp.bfloat16), "dp", scatter_dimension=2, tiled=True
        ).astype(jnp.float32),
    )
    return (
        layer_out,
        grad_tokens,
        grad_gates,
        grad_gain_attn,
        grad_gain_ffn,
        grad_query,
        grad_key,
        grad_value,
        grad_out,
        grad_gate,
        grad_up,
        grad_down,
    )


def solution(mesh):
    in_specs = (
        P(("dp", "tensor"), None),
        P(),
        P(),
        P("dp", "tensor"),
        P("dp", "tensor"),
        P("dp", "tensor"),
        P("tensor", "dp"),
        P("tensor", "dp", None),
        P("tensor", "dp", None),
        P("tensor", None, "dp"),
        P("dp", None),
        P("dp", None),
        P(("dp", "tensor"), None),
    )
    out_specs = (
        P(("dp", "tensor"), None),
        P(("dp", "tensor"), None),
        P(("dp", "tensor"), None),
        P(),
        P(),
        P("dp", "tensor"),
        P("dp", "tensor"),
        P("dp", "tensor"),
        P("tensor", "dp"),
        P("tensor", "dp", None),
        P("tensor", "dp", None),
        P("tensor", None, "dp"),
    )
    return jax.shard_map(
        on_device, mesh=mesh, in_specs=in_specs, out_specs=out_specs, check_vma=False
    )
```

profile of v0, /device:TPU:0, one launch (start us, length us, event | category | flops | bytes accessed | tf_op | source)
XLA Modules:
  0.0 1595.6 jit_solution(14270862726724773425)
XLA Ops:
  9.0 2.0 fusion.26
  12.7 24.8 %all_gather.42 = bf16[1024,256]{1,0:T(8,128)(2,1)S(1)} all-gather(bf16[64,256]{1,0:T(8,128)(2,1)} %param.17), channel_id=1, replica_groups=mesh['dp'=16,'tensor'=2] {'dp'}, dimensions={0}, use_global_device_ids=true | all-gather | bytes 557056 | tf_op jit(solution)/shard_map/all_gather | solution.py:218
  37.5 19.2 %all_gather.41 = bf16[1024,256]{1,0:T(8,128)(2,1)S(1)} all-gather(bf16[64,256]{1,0:T(8,128)(2,1)} %param.18), channel_id=1, replica_groups=mesh['dp'=16,'tensor'=2] {'dp'}, dimensions={0}, use_global_device_ids=true | all-gather | bytes 557056 | tf_op jit(solution)/shard_map/all_gather | solution.py:219
  57.1 1.8 fusion.64
  59.1 2.5 convolution_convert_fusion.9
  61.6 14.5 all-gather.12.cloned.1.call-done
  76.1 2.0 fusion.65
  80.0 1.8 exponential_reduce_fusion
  83.3 2.3 convolution_convert_fusion.7
  85.6 29.5 %all-gather.14.cloned.1.call-done = bf16[512,1024]{0,1:T(8,128)(2,1)} async-done(((bf16[512,64]{0,1:T(8,128)(2,1)}), bf16[512,1024]{0,1:T(8,128)(2,1)}) %all-gather.14.cloned.1.call-update) | async-done | bytes 1048592 | tf_op jit(solution)/shard_map/all_gather | solution.py:220
  115.2 3.3 fusion.66
  119.2 30.3 %reduce-scatter.13.cloned.1.call-done = f32[256,1024]{1,0:T(8,128)} async-done(((f32[512,1024]{1,0:T(8,128)}), f32[256,1024]{1,0:T(8,128)}) %reduce-scatter.13.cloned.1.call-update) | async-done | bytes 1048592 | tf_op jit(solution)/shard_map/reduce_scatter | solution.py:63
  155.8 4.6 reduce-window.6
  162.2 15.5 scatter_custom_fusion
  178.1 13.6 gather_fusion
  192.4 13.4 gather_fusion.2
  205.8 13.6 gather_fusion.1
  219.4 105.5 %all-gather.20.cloned.1.call-done = bf16[16,1024,512]{2,1,0:T(8,128)(2,1)} async-done(((bf16[16,64,512]{2,1,0:T(8,128)(2,1)}), bf16[16,1024,512]{2,1,0:T(8,128)(2,1)}) %all-gather.20.cloned.1.call-update) | async-done | bytes 16777232 | tf_op jit(solution)/shard_map/all_gather | solution.py:252
  325.0 12.6 fusion.13
  337.6 114.9 %all-gather.18.cloned.1.call-done = bf16[16,1024,512]{2,1,0:T(8,128)(2,1)} async-done(((bf16[16,64,512]{2,1,0:T(8,128)(2,1)}), bf16[16,1024,512]{2,1,0:T(8,128)(2,1)}) %all-gather.18.cloned.1.call-update) | async-done | bytes 16777232 | tf_op jit(solution)/shard_map/all_gather | solution.py:251
  452.5 12.6 fusion.15
  465.1 114.9 %all-gather.22.cloned.1.call-done = bf16[16,512,1024]{1,2,0:T(8,128)(2,1)} async-done(((bf16[16,512,64]{1,2,0:T(8,128)(2,1)}), bf16[16,512,1024]{1,2,0:T(8,128)(2,1)}) %all-gather.22.cloned.1.call-update) | async-done | bytes 16777232 | tf_op jit(solution)/shard_map/all_gather | solution.py:253
  580.0 16.1 %multiply_convert_fusion = (bf16[16,160,512]{2,1,0:T(8,128)(2,1)}, bf16[16,160,512]{2,1,0:T(8,128)(2,1)S(1)}, bf16[16,160,512]{2,1,0:T(8,128)(2,1)S(1)}) fusion(f32[16,160,512]{2,1,0:T(8,128)} %fusion.15, f32[16,160,512]{2,1,0:T(8,128)} %fusion.13, bf16[16,512,1024]{1,2,0:T(8,128)(2,1)} %all-gather.22.cloned.1.call-done, ...), kind=kOutput, calls=%fused_computation.25 | convolution fusion | flops 2711879680 | bytes 40380416 | tf_op jit(solution)/shard_map/ecd,efd->ecf/dot_general | solution.py:294
  596.1 12.4 fusion.67
  608.5 14.8 convolution_add_fusion
  623.3 8.8 bitcast_multiply_fusion
  632.1 24.7 %scatter_custom_fusion.2 = f32[512,1024]{1,0:T(8,128)} fusion(s32[2560]{0:T(1024)S(1)} %get-tuple-element.95, f32[2560,1024]{1,0:T(8,128)} %bitcast_multiply_fusion, f32[]{:T(128)} %constant.114.clone.1), kind=kCustom, calls=%fused_computation.82 | custom fusion | flops 2621440 | bytes 2097664 | tf_op jit(solution)/shard_map/scatter-add | solution.py:316
  656.9 30.1 %reduce-scatter.17.cloned.1.call-done = f32[256,1024]{1,0:T(8,128)} async-done(((f32[512,1024]{1,0:T(8,128)}), f32[256,1024]{1,0:T(8,128)}) %reduce-scatter.17.cloned.1.call-update) | async-done | bytes 1048592 | tf_op jit(solution)/shard_map/reduce_scatter | solution.py:326
  687.0 2.5 multiply_reduce_fusion
  689.5 2.6 fusion.60
  692.3 12.8 fusion.1
  705.2 17.9 %scatter_custom_fusion.3 = f32[4097]{0:T(1024)S(1)} fusion(s32[2560]{0:T(1024)S(1)} %get-tuple-element.96, f32[2560]{0:T(1024)S(1)} %broadcast_select_fusion.1, f32[]{:T(128)} %constant.114.clone.1), kind=kCustom, calls=%fused_computation.124 | custom fusion | flops 2560 | bytes 16392 | tf_op jit(solution)/shard_map/scatter-add | solution.py:322
  724.2 2.3 convolution_convert_fusion.8
  726.6 5.7 fusion.25
  732.2 5.3 fusion.2
  737.6 2.7 fusion.4
  740.3 2.0 copy-done.1
  742.3 2.2 broadcast_multiply_fusion
  748.0 2.5 convolution_convert_fusion.6
  750.5 4.1 fusion.68
  757.6 1.7 convolution_convert_fusion.4
  759.4 3.2 convolution_convert_fusion.3
  764.2 2.2 fusion.69
  766.4 1.8 add_add_fusion
  768.5 8.8 bitcast_multiply_fusion.1
  777.3 24.7 %scatter_custom_fusion.1 = f32[512,1024]{1,0:T(8,128)} fusion(s32[2560]{0:T(1024)} %copy-done.35, f32[2560,1024]{1,0:T(8,128)} %bitcast_multiply_fusion.1, f32[]{:T(128)} %constant.114.clone.1), kind=kCustom, calls=%fused_computation.84 | custom fusion | flops 2621440 | bytes 2097664 | tf_op jit(solution)/shard_map/scatter-add | solution.py:272
  802.0 2.7 convert_element_type.199
  804.8 11.1 convolution_convert_fusion.2
  815.9 11.0 convolution_convert_fusion.1
  827.7 11.8 convolution_convert_fusion
  839.6 1.7 copy.38
  842.7 18.0 %reduce-scatter.25.cloned.1.call-done = bf16[64,256]{1,0:T(8,128)(2,1)} async-done(((bf16[1024,256]{1,0:T(8,128)(2,1)}), bf16[64,256]{1,0:T(8,128)(2,1)}) %reduce-scatter.25.cloned.1.call-update) | async-done | bytes 32784 | tf_op jit(solution)/shard_map/reduce_scatter | solution.py:380
  862.1 59.0 %reduce-scatter.23.cloned.1.call-done = bf16[64,512]{1,0:T(8,128)(2,1)} async-done(((bf16[1024,512]{1,0:T(8,128)(2,1)}), bf16[64,512]{1,0:T(8,128)(2,1)}) %reduce-scatter.23.cloned.1.call-update) | async-done | bytes 65552 | tf_op jit(solution)/shard_map/reduce_scatter | solution.py:377
  922.6 58.5 %reduce-scatter.29.cloned.1.call-done = bf16[512,64]{0,1:T(8,128)(2,1)} async-done(((bf16[512,1024]{0,1:T(8,128)(2,1)}), bf16[512,64]{0,1:T(8,128)(2,1)}) %reduce-scatter.29.cloned.1.call-update) | async-done | bytes 65552 | tf_op jit(solution)/shard_map/reduce_scatter | solution.py:386
  982.6 32.1 %reduce-scatter.19.cloned.1.call-done = f32[256,1024]{1,0:T(8,128)} async-done(((f32[512,1024]{1,0:T(8,128)}), f32[256,1024]{1,0:T(8,128)}) %reduce-scatter.19.cloned.1.call-update) | async-done | bytes 1048592 | tf_op jit(solution)/shard_map/reduce_scatter | solution.py:63
  1014.6 1.7 fusion.31
  1016.3 39.6 %all-reduce = (f32[1024]{0:T(1024)}, f32[1024]{0:T(1024)}) all-reduce(f32[1024]{0:T(1024)S(1)} %get-tuple-element.71, f32[1024]{0:T(1024)S(1)} %copy-done.37), channel_id=1, replica_groups=mesh['dp'=16,'tensor'=2] {'dp','tensor'}, use_global_device_ids=true, to_apply=%region_21.22 | all-reduce | flops 2048 | bytes 16384 | tf_op jit(solution)/shard_map/psum | solution.py:375
  1056.0 3.3 fusion.30
  1059.3 161.8 %reduce-scatter.31.cloned.1.call-done = bf16[16,64,512]{2,1,0:T(8,128)(2,1)} async-done(((bf16[16,1024,512]{2,1,0:T(8,128)(2,1)}), bf16[16,64,512]{2,1,0:T(8,128)(2,1)}) %reduce-scatter.31.cloned.1.call-update) | async-done | bytes 1048592 | tf_op jit(solution)/shard_map/reduce_scatter | solution.py:391
  1221.1 2.8 convert_element_type.226
  1223.9 179.3 %reduce-scatter.33.cloned.1.call-done = bf16[16,64,512]{2,1,0:T(8,128)(2,1)} async-done(((bf16[16,1024,512]{2,1,0:T(8,128)(2,1)}), bf16[16,64,512]{2,1,0:T(8,128)(2,1)}) %reduce-scatter.33.cloned.1.call-update) | async-done | bytes 1048592 | tf_op jit(solution)/shard_map/reduce_scatter | solution.py:394
  1403.2 2.8 convert_element_type.228
  1406.1 179.4 %reduce-scatter.35.cloned.1.call-done = bf16[16,512,64]{1,2,0:T(8,128)(2,1)} async-done(((bf16[16,512,1024]{1,2,0:T(8,128)(2,1)}), bf16[16,512,64]{1,2,0:T(8,128)(2,1)}) %reduce-scatter.35.cloned.1.call-update) | async-done | bytes 1048592 | tf_op jit(solution)/shard_map/reduce_scatter | solution.py:397
  1585.5 2.8 convert_element_type.230
  (200 shorter events, 33.3 us)
Async XLA Ops:
  7.2 49.9 %all-gather.10.cloned.1.call-start = ((), (), s32[]{:S(2)}) async-start(), calls=%async_computation.12 | async-start | bytes 1572864 | tf_op jit(solution)/shard_map/all_gather | solution.py:59
  11.1 65.0 %all-gather.12.cloned.1.call-start = ((), (), s32[]{:S(2)}) async-start(), calls=%async_computation.13 | async-start | bytes 1114112 | tf_op jit(solution)/shard_map/all_gather | solution.py:217
  11.8 103.3 %all-gather.14.cloned.1.call-start = ((), (), s32[]{:S(2)}) async-start(), calls=%async_computation.14 | async-start | bytes 1114112 | tf_op jit(solution)/shard_map/all_gather | solution.py:220
  12.6 136.9 %reduce-scatter.13.cloned.1.call-start = ((), (), s32[]{:S(2)}) async-start(), calls=%async_computation.15 | async-start | bytes 3145728 | tf_op jit(solution)/shard_map/reduce_scatter | solution.py:63
  37.5 40.6 %copy-start.18 = (bf16[1024,256]{1,0:T(8,128)(2,1)}, bf16[1024,256]{1,0:T(8,128)(2,1)S(1)}, u32[]{:S(2)}) copy-start(bf16[1024,256]{1,0:T(8,128)(2,1)S(1)} %all_gather.42) | copy-start | bytes 1572868
  56.7 21.4 %copy-start.16 = (bf16[1024,256]{1,0:T(8,128)(2,1)}, bf16[1024,256]{1,0:T(8,128)(2,1)S(1)}, u32[]{:S(2)}) copy-start(bf16[1024,256]{1,0:T(8,128)(2,1)S(1)} %all_gather.41) | copy-start | bytes 1572868
  57.0 21.2 %copy-start.14 = (f32[512,64]{0,1:T(8,128)}, f32[512,64]{0,1:T(8,128)S(1)}, u32[]{:S(2)}) copy-start(f32[512,64]{0,1:T(8,128)S(1)} %get-tuple-element.111) | copy-start | bytes 393220
  57.0 21.2 %copy-start.21 = (f32[512,64]{0,1:T(8,128)}, f32[512,64]{0,1:T(8,128)S(1)}, u32[]{:S(2)}) copy-start(f32[512,64]{0,1:T(8,128)S(1)} %get-tuple-element.110) | copy-start | bytes 393220
  57.1 19.0 %copy-start.5 = (bf16[512,1024]{1,0:T(8,128)(2,1)S(1)}, bf16[512,1024]{1,0:T(8,128)(2,1)}, u32[]{:S(2)}) copy-start(bf16[512,1024]{1,0:T(8,128)(2,1)} %all-gather.10.cloned.1.call-done) | copy-start | bytes 3145732
  59.1 20.9 %copy-start.23 = (bf16[512,4,64,1]{0,2,3,1:T(8,128)(2,1)}, bf16[512,4,64,1]{0,2,3,1:T(8,128)(2,1)S(1)}, u32[]{:S(2)}) copy-start(bf16[512,4,64,1]{0,2,3,1:T(8,128)(2,1)S(1)} %fusion.44) | copy-start | bytes 786436
  78.5 1.5 copy-start.12
  80.0 3.3 copy-start
  80.0 3.2 copy-start.25
  85.6 67.2 %copy-start.29 = (bf16[4,64,2,512]{3,1,2,0:T(8,128)(2,1)}, bf16[4,64,2,512]{3,1,2,0:T(8,128)(2,1)S(1)}, u32[]{:S(2)}) copy-start(bf16[4,64,2,512]{3,1,2,0:T(8,128)(2,1)S(1)} %convolution_convert_fusion.7) | copy-start | bytes 1572868
  85.6 63.8 %copy-start.8 = (bf16[256,1024]{1,0:T(8,128)(2,1)S(1)}, bf16[256,1024]{1,0:T(8,128)(2,1)}, u32[]{:S(2)}) copy-start(bf16[256,1024]{1,0:T(8,128)(2,1)} %param.13) | copy-start | bytes 1572868
  85.6 66.2 %copy-start.34 = (f32[1024]{0:T(1024)S(1)}, f32[1024]{0:T(1024)}, u32[]{:S(2)}) copy-start(f32[1024]{0:T(1024)} %param.15) | copy-start | bytes 12292
  118.5 36.8 %copy-start.38 = (s32[512,8]{0,1:T(8,128)S(1)}, s32[512,8]{0,1:T(8,128)}, u32[]{:S(2)}) copy-start(s32[512,8]{0,1:T(8,128)} %param.24) | copy-start | bytes 49156
  118.5 73.9 %all-gather.24.cloned.1.call-start = ((), (), s32[]{:S(2)}) async-start(), calls=%async_computation.21 | async-start | bytes 1572864 | tf_op jit(solution)/shard_map/all_gather | solution.py:59
  119.1 58.7 %copy-start.39 = (f32[512,8]{0,1:T(8,128)S(1)}, f32[512,8]{0,1:T(8,128)}, u32[]{:S(2)}) copy-start(f32[512,8]{0,1:T(8,128)} %param.23) | copy-start | bytes 49156
  119.1 86.7 %all-gather.16.cloned.1.call-start = ((), (), s32[]{:S(2)}) async-start(), calls=%async_computation.16 | async-start | bytes 1572864 | tf_op jit(solution)/shard_map/all_gather | solution.py:59
  150.9 1.0 copy-start.3
  152.8 172.2 %all-gather.20.cloned.1.call-start = ((), (), s32[]{:S(2)}) async-start(), calls=%async_computation.18 | async-start | bytes 17825792 | tf_op jit(solution)/shard_map/all_gather | solution.py:252
  153.6 298.9 %all-gather.18.cloned.1.call-start = ((), (), s32[]{:S(2)}) async-start(), calls=%async_computation.17 | async-start | bytes 17825792 | tf_op jit(solution)/shard_map/all_gather | solution.py:251
  154.3 425.7 %all-gather.22.cloned.1.call-start = ((), (), s32[]{:S(2)}) async-start(), calls=%async_computation.19 | async-start | bytes 17825792 | tf_op jit(solution)/shard_map/all_gather | solution.py:253
  155.0 532.0 %reduce-scatter.17.cloned.1.call-start = ((), (), s32[]{:S(2)}) async-start(), calls=%async_computation.22 | async-start | bytes 3145728 | tf_op jit(solution)/shard_map/reduce_scatter | solution.py:326
  177.7 454.4 %copy-start.35 = (s32[2560]{0:T(1024)}, s32[2560]{0:T(1024)S(1)}, u32[]{:S(2)}) copy-start(s32[2560]{0:T(1024)S(1)} %get-tuple-element.95) | copy-start | bytes 30724
  192.4 387.7 %copy-start.30 = (f32[16,160]{1,0:T(8,128)}, f32[16,160]{1,0:T(8,128)S(1)}, u32[]{:S(2)}) copy-start(f32[16,160]{1,0:T(8,128)S(1)} %mul.334) | copy-start | bytes 30724
  596.1 12.4 copy-start.2
  632.1 57.4 %copy-start.19 = (bf16[256,1024]{1,0:T(8,128)(2,1)S(1)}, bf16[256,1024]{1,0:T(8,128)(2,1)}, u32[]{:S(2)}) copy-start(bf16[256,1024]{1,0:T(8,128)(2,1)} %param.25) | copy-start | bytes 1572868
  656.8 67.4 %all-gather.26.cloned.1.call-start = ((), (), s32[]{:S(2)}) async-start(), calls=%async_computation.23 | async-start | bytes 1572864 | tf_op jit(solution)/shard_map/all_gather | solution.py:59
  689.5 15.6 copy-start.42
  692.2 147.4 %reduce-scatter.21.cloned.1.call-start = ((), (), s32[]{:S(2)}) async-start(), calls=%async_computation.25 | async-start | bytes 393216 | tf_op jit(solution)/shard_map/reduce_scatter | solution.py:327
  724.0 117.3 %reduce-scatter.27.cloned.1.call-start = ((), (), s32[]{:S(2)}) async-start(), calls=%async_computation.28 | async-start | bytes 557056 | tf_op jit(solution)/shard_map/reduce_scatter | solution.py:383
  726.5 5.7 copy-start.26
  726.5 11.0 slice-start
  732.2 12.3 copy-start.27
  732.2 5.3 slice-start.1
  737.6 4.7 copy-start.13
  737.6 4.7 copy-start.15
  740.3 2.0 copy-start.1
  742.3 2.2 copy-start.6
  742.3 4.4 copy-start.22
  746.6 114.1 %reduce-scatter.25.cloned.1.call-start = ((), (), s32[]{:S(2)}) async-start(), calls=%async_computation.27 | async-start | bytes 557056 | tf_op jit(solution)/shard_map/reduce_scatter | solution.py:380
  754.7 166.4 %reduce-scatter.23.cloned.1.call-start = ((), (), s32[]{:S(2)}) async-start(), calls=%async_computation.26 | async-start | bytes 1114112 | tf_op jit(solution)/shard_map/reduce_scatter | solution.py:377
  754.7 1.8 copy-start.11
  754.7 2.8 copy-start.7
  756.8 0.8 copy-start.24
  759.3 7.0 copy-start.17
  759.4 221.7 %reduce-scatter.29.cloned.1.call-start = ((), (), s32[]{:S(2)}) async-start(), calls=%async_computation.29 | async-start | bytes 1114112 | tf_op jit(solution)/shard_map/reduce_scatter | solution.py:386
  762.6 252.0 %reduce-scatter.19.cloned.1.call-start = ((), (), s32[]{:S(2)}) async-start(), calls=%async_computation.24 | async-start | bytes 3145728 | tf_op jit(solution)/shard_map/reduce_scatter | solution.py:63
  762.6 3.8 copy-start.28
  766.4 2.1 copy-start.33
  768.3 287.7 %reduce-scatter.15.cloned.1.call-start = ((), (), s32[]{:S(2)}) async-start(), calls=%async_computation.20 | async-start | bytes 1572864 | tf_op jit(solution)/shard_map/reduce_scatter | solution.py:276
  804.7 416.4 %reduce-scatter.31.cloned.1.call-start = ((), (), s32[]{:S(2)}) async-start(), calls=%async_computation.30 | async-start | bytes 17825792 | tf_op jit(solution)/shard_map/reduce_scatter | solution.py:391
  815.9 587.4 %reduce-scatter.33.cloned.1.call-start = ((), (), s32[]{:S(2)}) async-start(), calls=%async_computation.31 | async-start | bytes 17825792 | tf_op jit(solution)/shard_map/reduce_scatter | solution.py:394
  827.0 758.5 %reduce-scatter.35.cloned.1.call-start = ((), (), s32[]{:S(2)}) async-start(), calls=%async_computation.32 | async-start | bytes 17825792 | tf_op jit(solution)/shard_map/reduce_scatter | solution.py:397
  839.5 175.1 %copy-start.9 = (bf16[256,1024]{1,0:T(8,128)(2,1)S(1)}, bf16[256,1024]{1,0:T(8,128)(2,1)}, u32[]{:S(2)}) copy-start(bf16[256,1024]{1,0:T(8,128)(2,1)} %param.13) | copy-start | bytes 1572868
  839.5 175.1 %copy-start.36 = (f32[1024]{0:T(1024)S(1)}, f32[1024]{0:T(1024)}, u32[]{:S(2)}) copy-start(f32[1024]{0:T(1024)} %param.14) | copy-start | bytes 12292
  839.5 175.1 %copy-start.41 = (f32[256]{0:T(256)S(1)}, f32[256]{0:T(256)}, u32[]{:S(2)}) copy-start(f32[256]{0:T(256)} %copy-done.40) | copy-start | bytes 3076
  839.5 176.8 %copy-start.37 = (f32[1024]{0:T(1024)S(1)}, f32[1024]{0:T(1024)}, u32[]{:S(2)}) copy-start(f32[1024]{0:T(1024)} %get-tuple-element.69) | copy-start | bytes 12292
  839.5 216.5 %copy-start.4 = (f32[256,1024]{1,0:T(8,128)S(1)}, f32[256,1024]{1,0:T(8,128)}, u32[]{:S(2)}) copy-start(f32[256,1024]{1,0:T(8,128)} %copy-done.3) | copy-start | bytes 3145732
  839.5 216.4 %copy-start.10 = (f32[256,1024]{1,0:T(8,128)S(1)}, f32[256,1024]{1,0:T(8,128)}, u32[]{:S(2)}) copy-start(f32[256,1024]{1,0:T(8,128)} %reduce-scatter.17.cloned.1.call-done) | copy-start | bytes 3145732
  839.5 216.4 %copy-start.20 = (bf16[256,1024]{1,0:T(8,128)(2,1)S(1)}, bf16[256,1024]{1,0:T(8,128)(2,1)}, u32[]{:S(2)}) copy-start(bf16[256,1024]{1,0:T(8,128)(2,1)} %param.25) | copy-start | bytes 1572868
  839.5 216.4 %copy-start.43 = (f32[256]{0:T(256)S(1)}, f32[256]{0:T(256)}, u32[]{:S(2)}) copy-start(f32[256]{0:T(256)} %copy-done.42) | copy-start | bytes 3076
  (3 other events, 1.9 us)
Sparse Core Ops, SparseCore 0:
  11.2 23.9 all-gather.9
  37.4 38.6 all-gather.11
  78.2 36.8 all-gather.13
  118.6 30.7 reduce-scatter.12
  150.9 21.3 all-gather.23
  174.3 21.2 all-gather.15
  198.0 126.8 all-gather.19
  327.4 125.0 all-gather.17
  454.9 125.0 all-gather.21
  657.0 30.0 reduce-scatter.16
  692.3 21.2 all-gather.25
  724.1 11.5 reduce-scatter.20
  746.8 55.6 reduce-scatter.26
  805.8 54.8 reduce-scatter.24
  864.6 56.3 reduce-scatter.22
  924.5 56.4 reduce-scatter.28
  983.8 30.7 reduce-scatter.18
  1017.3 20.5 reduce-scatter.14
  1042.5 178.5 reduce-scatter.30
  1225.6 177.5 reduce-scatter.32
  1407.9 177.5 reduce-scatter.34
where the time goes:
time: 1600 us
  waiting for transfers between devices  1130 us (71%)
  matrix products  162 us (10%)
  other arithmetic  133 us (8%)
  blocking collectives  83.6 us (5%)
  local copies, waits for them, and re-layouts  67.6 us (4%)
    reduce_scatter x1, waiting for transfers between devices, on_device(): lax.psum_scatter(grad_down_w.astype(jnp.bfloat16), 'dp', scatter_dimensio...  179 us
    reduce_scatter x1, waiting for transfers between devices, on_device(): lax.psum_scatter(grad_up_w.astype(jnp.bfloat16), 'dp', scatter_dimension=...  179 us
    reduce_scatter x1, waiting for transfers between devices, on_device(): lax.psum_scatter(grad_gate_w.astype(jnp.bfloat16), 'dp', scatter_dimensio...  162 us
    all_gather x1, waiting for transfers between devices, on_device(): lax.all_gather(w_down, 'dp', axis=2, tiled=True)  115 us
    all_gather x1, waiting for transfers between devices, on_device(): lax.all_gather(w_gate, 'dp', axis=1, tiled=True)  115 us
    all_gather x1, waiting for transfers between devices, on_device(): lax.all_gather(w_up, 'dp', axis=1, tiled=True)  106 us
    reduce_scatter x2, waiting for transfers between devices, sum_rows(): lax.psum_scatter(term(jnp.int32(0), lax.axis_size('tensor') * own_rows),...  62.3 us
    reduce_scatter x1, waiting for transfers between devices, on_device(): lax.psum_scatter(grad_query_w.astype(jnp.bfloat16), 'dp', scatter_dimensi...  59 us
  transfers between devices with their start and end apart: 21, of which 14 were waited for; matrix products, arithmetic and copies ran while one was open for 17% of the time, Pallas kernels for 0%

commit v1 on v0

--- a/solution.py
+++ b/solution.py
@@ -59,34 +59,32 @@
     return lax.all_gather(values, "tensor", axis=0, tiled=True)
 
 
-def sum_rows(term, own_rows):
-    return lax.psum_scatter(
-        term(jnp.int32(0), lax.axis_size("tensor") * own_rows),
-        "tensor",
-        scatter_dimension=0,
-        tiled=True,
-    )
-
-
-def dispatch(route_rows, first_expert, expert_count, capacity):
-    flat_routes = route_rows.reshape(-1)
-    offset_ids = flat_routes - first_expert
-    onehot = (offset_ids[:, None] == jnp.arange(expert_count, dtype=jnp.int32)[None, :]).astype(
-        jnp.int32
-    )
-    earlier = jnp.cumsum(onehot, 0) - onehot
-    slot_index = jnp.sum(earlier * onehot, 1)
-    owned = (offset_ids >= 0) & (offset_ids < expert_count)
-    position = jnp.where(owned, offset_ids * capacity + slot_index, expert_count * capacity)
-    numbers = jnp.arange(flat_routes.shape[0], dtype=jnp.int32) + 1
-    slot_table = (
-        jnp.zeros((expert_count * capacity + 1,), jnp.int32)
-        .at[position]
-        .set(numbers)[: expert_count * capacity]
-    )
-    filled = slot_table > 0
-    source = jnp.maximum(slot_table - 1, 0)
-    return (source // TOP, filled, source)
+def sum_rows(term):
+    size = lax.axis_size("tensor")
+    own_rows = term.shape[0] // size
+    if size != 2:
+        return lax.psum_scatter(term, "tensor", scatter_dimension=0, tiled=True)
+    index = lax.axis_index("tensor")
+    kept = lax.dynamic_slice_in_dim(term, index * own_rows, own_rows, 0)
+    sent = lax.dynamic_slice_in_dim(term, (1 - index) * own_rows, own_rows, 0)
+    received = lax.ppermute(sent.astype(jnp.bfloat16), "tensor", [(0, 1), (1, 0)])
+    return kept + received.astype(jnp.float32)
+
+
+def dispatch(route_rows, gate_rows, first_expert, expert_count, capacity):
+    rows = route_rows.shape[0]
+    experts = first_expert + jnp.arange(expert_count, dtype=jnp.int32)
+    pairs = route_rows[:, :, None] == experts[None, None, :]
+    named = jnp.any(pairs, 1)
+    row_gates = jnp.sum(jnp.where(pairs, gate_rows[:, :, None], 0.0), 1)
+    order = jnp.arange(rows, dtype=jnp.int32)
+    before = (order[None, :] < order[:, None]).astype(jnp.bfloat16)
+    rank = jnp.dot(
+        before, named.astype(jnp.bfloat16), preferred_element_type=jnp.float32
+    ).astype(jnp.int32)
+    rank = jnp.where(named, rank, capacity)
+    slots = rank[:, :, None] == jnp.arange(capacity, dtype=jnp.int32)[None, None, :]
+    return (pairs, row_gates, slots)
 
 
 def block_scores(block_queries, seq_keys, start_row, block_rows, seq_length):
@@ -212,19 +210,62 @@
     local_experts = w_gate.shape[0]
     head_count = w_query.shape[1] // HEAD_DIM
     kv_count = w_key.shape[1] // HEAD_DIM
+    query_width = w_query.shape[1]
+    key_width = w_key.shape[1]
+    pre_width = query_width + 2 * key_width
+    rows_shard = w_query.shape[0]
+    owns_experts = local_experts == lax.axis_size("dp")
     cosine, sine_table = rope_tables(group_rows, seq_length)
-    query_full, key_full, value_full, out_full = (
-        lax.all_gather(w_query, "dp", axis=0, tiled=True),
-        lax.all_gather(w_key, "dp", axis=0, tiled=True),
-        lax.all_gather(w_value, "dp", axis=0, tiled=True),
-        lax.all_gather(w_out, "dp", axis=1, tiled=True),
-    )
+    attn_full = lax.all_gather(
+        jnp.concatenate([w_query, w_key, w_value, w_out.T], 1), "dp", axis=0, tiled=True
+    )
+    pre_full = attn_full[:, :pre_width]
+    out_full = attn_full[:, pre_width:]
+    expert_stack = jnp.stack([w_gate, w_up, w_down.transpose(0, 2, 1)], 1)
+    if owns_experts:
+        expert_full = lax.all_to_all(expert_stack, "dp", split_axis=0, concat_axis=0, tiled=True)
+        gate_full, up_full, down_full = (
+            expert_full[:, index].reshape(1, D, expert_stack.shape[3]) for index in range(3)
+        )
+    else:
+        expert_full = lax.all_gather(expert_stack, "dp", axis=2, tiled=True)
+        gate_full, up_full, down_full = (expert_full[:, index] for index in range(3))
+
+    def to_experts(rows):
+        if not owns_experts:
+            return rows.reshape(local_experts, capacity, D)
+        moved = lax.all_to_all(
+            rows.reshape(local_experts, capacity, D), "dp", split_axis=0, concat_axis=0, tiled=True
+        )
+        return moved.reshape(1, local_experts * capacity, D)
+
+    def from_experts(rows):
+        if not owns_experts:
+            return rows.reshape(-1, D)
+        moved = lax.all_to_all(
+            rows.reshape(local_experts, capacity, D), "dp", split_axis=0, concat_axis=0, tiled=True
+        )
+        return moved.reshape(-1, D)
+
+    pairs, row_gates, slots = dispatch(
+        routes, route_gates, lax.axis_index("tensor") * local_experts, local_experts, capacity
+    )
+    slot_rows = slots.reshape(group_rows, -1).astype(jnp.bfloat16)
+    gated_rows = (
+        jnp.where(slots, row_gates[:, :, None], 0.0).astype(jnp.bfloat16).reshape(group_rows, -1)
+    )
+    slot_gate = jnp.sum(jnp.where(slots, row_gates[:, :, None], 0.0), 0).reshape(-1)
+    grad_full = spread(cotangent)
+    grad_slots = jnp.einsum("ts,td->sd", slot_rows, grad_full, preferred_element_type=jnp.float32)
+    grad_expert = to_experts((slot_gate[:, None] * grad_slots).astype(jnp.bfloat16))
+
     token_values = tokens.astype(jnp.float32)
     normed_own, scaled_attn, factor_attn = normalize(token_values, gain_attn)
     normed = spread(normed_own)
-    query_pre = jnp.dot(normed, query_full, preferred_element_type=jnp.float32)
-    key_pre = jnp.dot(normed, key_full, preferred_element_type=jnp.float32)
-    value_pre = jnp.dot(normed, value_full, preferred_element_type=jnp.float32)
+    pre = jnp.dot(normed, pre_full, preferred_element_type=jnp.float32)
+    query_pre = pre[:, :query_width]
+    key_pre = pre[:, query_width : query_width + key_width]
+    value_pre = pre[:, query_width + key_width :]
     queries = rotate(
         query_pre.reshape(group_rows, head_count, HEAD_DIM), cosine, sine_table
     ).astype(jnp.bfloat16)
@@ -236,109 +277,85 @@
         queries, key_rows, value_rows, seq_length, block_rows
     )
     mixed = attended_values.astype(jnp.bfloat16)
-
-    def out_term(start_row, row_span):
-        return jnp.dot(
-            lax.dynamic_slice_in_dim(mixed, start_row, row_span, 0),
-            out_full,
-            preferred_element_type=jnp.float32,
-        )
-
-    attended = token_values + sum_rows(out_term, own_rows)
+    attended = token_values + sum_rows(
+        jnp.einsum("tc,dc->td", mixed, out_full, preferred_element_type=jnp.float32)
+    )
     routed_own, scaled_ffn, factor_ffn = normalize(attended, gain_ffn)
     routed = spread(routed_own)
-    gate_full, up_full, down_full = (
-        lax.all_gather(w_gate, "dp", axis=1, tiled=True),
-        lax.all_gather(w_up, "dp", axis=1, tiled=True),
-        lax.all_gather(w_down, "dp", axis=2, tiled=True),
-    )
-    token_index, filled, source = dispatch(
-        routes, lax.axis_index("tensor") * local_experts, local_experts, capacity
-    )
-    filled_rows = filled.astype(jnp.float32)
-    slot_gate = route_gates.reshape(-1)[source] * filled_rows
-    expert_in = (routed[token_index] * filled.astype(jnp.bfloat16)[:, None]).reshape(
-        local_experts, capacity, D
+    expert_in = to_experts(
+        jnp.einsum("ts,td->sd", slot_rows, routed, preferred_element_type=jnp.float32).astype(
+            jnp.bfloat16
+        )
     )
     gate_pre = jnp.einsum("ecd,edf->ecf", expert_in, gate_full, preferred_element_type=jnp.float32)
     up_pre = jnp.einsum("ecd,edf->ecf", expert_in, up_full, preferred_element_type=jnp.float32)
     sigmoid_gate = jax.nn.sigmoid(gate_pre)
     silu_gate = gate_pre * sigmoid_gate
     hidden = (silu_gate * up_pre).astype(jnp.bfloat16)
-    expert_out = jnp.einsum(
-        "ecf,efd->ecd", hidden, down_full, preferred_element_type=jnp.float32
-    ).reshape(-1, D)
-    combined = (
-        jnp.zeros((group_rows, D), jnp.float32).at[token_index].add(slot_gate[:, None] * expert_out)
-    )
-    layer_out = (
-        attended
-        + lax.psum_scatter(
-            combined.astype(jnp.bfloat16), "tensor", scatter_dimension=0, tiled=True
-        ).astype(jnp.float32)
-    ).astype(jnp.bfloat16)
-    grad_full = spread(cotangent)
-    gate_full, up_full, down_full = (
-        lax.all_gather(w_gate, "dp", axis=1, tiled=True),
-        lax.all_gather(w_up, "dp", axis=1, tiled=True),
-        lax.all_gather(w_down, "dp", axis=2, tiled=True),
-    )
-    grad_slots = grad_full[token_index].astype(jnp.float32)
-    gate_grad = jnp.sum(grad_slots * expert_out, -1) * filled_rows
-    grad_expert = (
-        (slot_gate[:, None] * grad_slots).astype(jnp.bfloat16).reshape(local_experts, capacity, D)
-    )
-    grad_down_w = jnp.einsum(
-        "ecf,ecd->efd", hidden, grad_expert, preferred_element_type=jnp.float32
+    expert_out = from_experts(
+        jnp.einsum("ecf,edf->ecd", hidden, down_full, preferred_element_type=jnp.float32).astype(
+            jnp.bfloat16
+        )
     )
     grad_hidden = jnp.einsum(
-        "ecd,efd->ecf", grad_expert, down_full, preferred_element_type=jnp.float32
+        "ecd,edf->ecf", grad_expert, down_full, preferred_element_type=jnp.float32
     )
     grad_gate_pre = (
         grad_hidden * up_pre * sigmoid_gate * (1.0 + gate_pre * (1.0 - sigmoid_gate))
     ).astype(jnp.bfloat16)
     grad_up_pre = (grad_hidden * silu_gate).astype(jnp.bfloat16)
-    grad_gate_w = jnp.einsum(
-        "ecd,ecf->edf", expert_in, grad_gate_pre, preferred_element_type=jnp.float32
-    )
-    grad_up_w = jnp.einsum(
-        "ecd,ecf->edf", expert_in, grad_up_pre, preferred_element_type=jnp.float32
-    )
     grad_expert_in = jnp.einsum(
         "ecf,edf->ecd", grad_gate_pre, gate_full, preferred_element_type=jnp.float32
     )
     grad_expert_in = grad_expert_in + jnp.einsum(
         "ecf,edf->ecd", grad_up_pre, up_full, preferred_element_type=jnp.float32
     )
-    routed_part = (
-        jnp.zeros((group_rows, D), jnp.float32)
-        .at[token_index]
-        .add(grad_expert_in.reshape(-1, D) * filled_rows[:, None])
-    )
-    gate_slots = jnp.where(filled, source, group_rows * TOP)
-    gate_part = (
-        jnp.zeros((group_rows * TOP + 1,), jnp.float32)
-        .at[gate_slots]
-        .add(gate_grad)[: group_rows * TOP]
-        .reshape(group_rows, TOP)
-    )
-    grad_routed, grad_gates = (
-        lax.psum_scatter(routed_part, "tensor", scatter_dimension=0, tiled=True),
-        lax.psum_scatter(gate_part, "tensor", scatter_dimension=0, tiled=True),
-    )
+    routed_slots = from_experts(grad_expert_in.astype(jnp.bfloat16))
+    grad_stack = jnp.stack(
+        [
+            jnp.einsum("ecd,ecf->edf", left, right, preferred_element_type=jnp.float32).astype(
+                jnp.bfloat16
+            )
+            for left, right in (
+                (expert_in, grad_gate_pre),
+                (expert_in, grad_up_pre),
+                (grad_expert, hidden),
+            )
+        ],
+        1,
+    )
+    if owns_experts:
+        grad_shards = lax.all_to_all(
+            grad_stack.reshape(3, local_experts, rows_shard, -1).transpose(1, 0, 2, 3),
+            "dp",
+            split_axis=0,
+            concat_axis=0,
+            tiled=True,
+        )
+    else:
+        grad_shards = lax.psum_scatter(grad_stack, "dp", scatter_dimension=2, tiled=True)
+    grad_shards = grad_shards.astype(jnp.float32)
+    grad_gate, grad_up = (grad_shards[:, 0], grad_shards[:, 1])
+    grad_down = grad_shards[:, 2].transpose(0, 2, 1)
+
+    routed_part = jnp.dot(slot_rows, routed_slots, preferred_element_type=jnp.float32)
+    grad_routed = sum_rows(routed_part)
+    combined = jnp.dot(gated_rows, expert_out, preferred_element_type=jnp.float32)
+    layer_out = (attended + sum_rows(combined)).astype(jnp.bfloat16)
+    gate_grad = jnp.sum(grad_slots * expert_out.astype(jnp.float32), -1)
+    row_grads = jnp.sum(
+        jnp.where(slots, gate_grad.reshape(1, local_experts, capacity), 0.0), -1
+    )
+    gate_part = jnp.sum(jnp.where(pairs, row_grads[:, None, :], 0.0), -1)
+    grad_gates = lax.psum_scatter(gate_part, "tensor", scatter_dimension=0, tiled=True)
+
     gain_ffn_part, attended_norm = normalize_back(grad_routed, scaled_ffn, factor_ffn, gain_ffn)
     grad_attended = cotangent.astype(jnp.float32) + attended_norm
     grad_branch = spread(grad_attended.astype(jnp.bfloat16))
-    query_full, key_full, value_full, out_full = (
-        lax.all_gather(w_query, "dp", axis=0, tiled=True),
-        lax.all_gather(w_key, "dp", axis=0, tiled=True),
-        lax.all_gather(w_value, "dp", axis=0, tiled=True),
-        lax.all_gather(w_out, "dp", axis=1, tiled=True),
-    )
-    grad_out_w = jnp.einsum("tc,td->cd", mixed, grad_branch, preferred_element_type=jnp.float32)
-    grad_mixed = jnp.einsum(
-        "td,cd->tc", grad_branch, out_full, preferred_element_type=jnp.float32
-    ).astype(jnp.bfloat16)
+    grad_out_w = jnp.einsum("td,tc->dc", grad_branch, mixed, preferred_element_type=jnp.float32)
+    grad_mixed = jnp.dot(grad_branch, out_full, preferred_element_type=jnp.float32).astype(
+        jnp.bfloat16
+    )
     grad_queries, grad_keys, grad_values = attend_backward(
         queries, key_rows, value_rows, grad_mixed, log_sums, seq_length, block_rows
     )
@@ -348,56 +365,30 @@
     grad_key_pre = (
         rotate_back(grad_keys, cosine, sine_table).astype(jnp.bfloat16).reshape(group_rows, -1)
     )
-    grad_value_pre = grad_values.astype(jnp.bfloat16)
-    grad_query_w = jnp.einsum(
-        "td,tc->dc", normed, grad_query_pre, preferred_element_type=jnp.float32
-    )
-    grad_key_w = jnp.einsum("td,tc->dc", normed, grad_key_pre, preferred_element_type=jnp.float32)
-    grad_value_w = jnp.einsum(
-        "td,tc->dc", normed, grad_value_pre, preferred_element_type=jnp.float32
-    )
-
-    def input_term(start_row, row_span):
-        value_piece = lax.dynamic_slice_in_dim(grad_value_pre, start_row, row_span, 0)
-        partial_sum = jnp.einsum(
-            "tc,dc->td", grad_query_pre, query_full, preferred_element_type=jnp.float32
-        )
-        partial_sum = partial_sum + jnp.einsum(
-            "tc,dc->td", grad_key_pre, key_full, preferred_element_type=jnp.float32
-        )
-        return partial_sum + jnp.einsum(
-            "tc,dc->td", value_piece, value_full, preferred_element_type=jnp.float32
-        )
-
-    grad_normed = sum_rows(input_term, own_rows)
+    grad_pre = jnp.concatenate([grad_query_pre, grad_key_pre, grad_values.astype(jnp.bfloat16)], 1)
+    grad_pre_w = jnp.einsum("td,tc->dc", normed, grad_pre, preferred_element_type=jnp.float32)
+    grad_normed = sum_rows(
+        jnp.einsum("tc,dc->td", grad_pre, pre_full, preferred_element_type=jnp.float32)
+    )
     gain_attn_part, tokens_norm = normalize_back(grad_normed, scaled_attn, factor_attn, gain_attn)
     grad_tokens = grad_attended + tokens_norm
-    grad_gain_attn, grad_gain_ffn = lax.psum((gain_attn_part, gain_ffn_part), ("dp", "tensor"))
-    grad_query, grad_key, grad_value, grad_out = (
-        lax.psum_scatter(
-            grad_query_w.astype(jnp.bfloat16), "dp", scatter_dimension=0, tiled=True
-        ).astype(jnp.float32),
-        lax.psum_scatter(
-            grad_key_w.astype(jnp.bfloat16), "dp", scatter_dimension=0, tiled=True
-        ).astype(jnp.float32),
-        lax.psum_scatter(
-            grad_value_w.astype(jnp.bfloat16), "dp", scatter_dimension=0, tiled=True
-        ).astype(jnp.float32),
-        lax.psum_scatter(
-            grad_out_w.astype(jnp.bfloat16), "dp", scatter_dimension=1, tiled=True
-        ).astype(jnp.float32),
-    )
-    grad_gate, grad_up, grad_down = (
-        lax.psum_scatter(
-            grad_gate_w.astype(jnp.bfloat16), "dp", scatter_dimension=1, tiled=True
-        ).astype(jnp.float32),
-        lax.psum_scatter(
-            grad_up_w.astype(jnp.bfloat16), "dp", scatter_dimension=1, tiled=True
-        ).astype(jnp.float32),
-        lax.psum_scatter(
-            grad_down_w.astype(jnp.bfloat16), "dp", scatter_dimension=2, tiled=True
-        ).astype(jnp.float32),
-    )
+    gain_parts = lax.all_gather(
+        jnp.stack([gain_attn_part, gain_ffn_part]), ("dp", "tensor"), axis=0, tiled=False
+    )
+    gain_sums = jnp.sum(gain_parts, 0)
+    grad_gain_attn, grad_gain_ffn = (gain_sums[0], gain_sums[1])
+    attn_shards = lax.psum_scatter(
+        jnp.concatenate(
+            [grad_pre_w.astype(jnp.bfloat16), grad_out_w.astype(jnp.bfloat16)], 1
+        ),
+        "dp",
+        scatter_dimension=0,
+        tiled=True,
+    ).astype(jnp.float32)
+    grad_query = attn_shards[:, :query_width]
+    grad_key = attn_shards[:, query_width : query_width + key_width]
+    grad_value = attn_shards[:, query_width + key_width : pre_width]
+    grad_out = attn_shards[:, pre_width:].T
     return (
         layer_out,
         grad_tokens,

time: 1600 us -> 928 us (0.58)
  waiting for transfers between devices: 1130 us -> 430 us
  blocking collectives: 83.6 us -> 224 us
  other arithmetic: 133 us -> 41.6 us
  starting transfers between devices: 1.7 us -> 70.8 us
  matrix products: 162 us -> 106 us
  local copies, waits for them, and re-layouts: 67.6 us -> 29.4 us
    reduce_scatter x11 -> x0, waiting for transfers between devices: 748 us -> none  [the longest x1 179 us: on_device(): lax.psum_scatter(grad_down_w.astype(jnp.bfloat16), 'dp', scatter_dimensio...]
    all_gather x5 -> x1, waiting for transfers between devices: 379 us -> 71.8 us  [on_device(): lax.all_gather(jnp.concatenate([w_query, w_key, w_value, w_out.T], 1), 'd...]
    all_to_all x0 -> x5, waiting for transfers between devices: none -> 287 us  [the longest x2 160 us: from_experts(): lax.all_to_all(rows.reshape(local_experts, capacity, D), 'dp', split_axis...]
    all_to_all x0 -> x1, blocking collectives: none -> 139 us  [to_experts(): lax.all_to_all(rows.reshape(local_experts, capacity, D), 'dp', split_axis...]
    scatter-add x3 -> x0, other arithmetic: 67.3 us -> none  [the longest x1 24.7 us: on_device(): routed_part = jnp.zeros((group_rows, D), jnp.float32).at[token_index].add...]
    all_to_all x0 -> x5, starting transfers between devices: none -> 66.7 us  [the longest x2 29.4 us: from_experts(): lax.all_to_all(rows.reshape(local_experts, capacity, D), 'dp', split_axis...]
    all_gather x4, waiting for transfers between devices: 0.06 us -> 50.4 us  [spread(): return lax.all_gather(values, 'tensor', axis=0, tiled=True)]
    all_gather x2 -> x1, blocking collectives: 44 us -> 85.9 us  [on_device(): lax.all_gather(jnp.stack([gain_attn_part, gain_ffn_part]), ('dp', 'tensor...]
  transfers between devices with their start and end apart: 21 -> 16, of which waited for: 14 -> 11; matrix products, arithmetic and copies ran while one was open for 17% -> 12% of each run, Pallas kernels for 0% -> 0%
where the time goes in v1:
time: 928 us; the launch traced here: 917 us
  waiting for transfers between devices  430 us (46%)
  blocking collectives  224 us (24%)
  matrix products  106 us (11%)
  starting transfers between devices  70.8 us (8%)
  other arithmetic  41.6 us (4%)
  local copies, waits for them, and re-layouts  29.4 us (3%)
  between operations  15.6 us (2%)
    all_to_all x2, waiting for transfers between devices, from_experts(): lax.all_to_all(rows.reshape(local_experts, capacity, D), 'dp', split_axis...  160 us
    all_to_all x1, blocking collectives, to_experts(): lax.all_to_all(rows.reshape(local_experts, capacity, D), 'dp', split_axis...  139 us
    all_to_all x1, waiting for transfers between devices, to_experts(): lax.all_to_all(rows.reshape(local_experts, capacity, D), 'dp', split_axis...  92.3 us
    all_gather x1, blocking collectives, on_device(): lax.all_gather(jnp.stack([gain_attn_part, gain_ffn_part]), ('dp', 'tensor...  85.9 us
    all_gather x1, waiting for transfers between devices, on_device(): lax.all_gather(jnp.concatenate([w_query, w_key, w_value, w_out.T], 1), 'd...  71.8 us
    all_gather x4, waiting for transfers between devices, spread(): return lax.all_gather(values, 'tensor', axis=0, tiled=True)  50.4 us
    all_to_all x1, waiting for transfers between devices, on_device(): lax.all_to_all(grad_stack.reshape(3, local_experts, rows_shard, -1).trans...  34.4 us
    all_to_all x2, starting transfers between devices, from_experts(): lax.all_to_all(rows.reshape(local_experts, capacity, D), 'dp', split_axis...  29.4 us
  transfers between devices with their start and end apart: 16, of which 11 were waited for; matrix products, arithmetic and copies ran while one was open for 12% of the time, Pallas kernels for 0%

profile of v1, /device:TPU:0, one launch (start us, length us, event | category | flops | bytes accessed | tf_op | source)
XLA Modules:
  0.0 917.4 jit_solution(15881892710625739139)
XLA Ops:
  7.2 1.2 fusion.31
  8.5 2.0 fusion.25
  10.6 1.6 pad_maximum_fusion.6
  12.2 3.9 pad_maximum_fusion
  16.1 7.4 all-to-all-start.1
  24.0 10.7 %all-gather.8.cloned.1.call-done = bf16[512,1024]{1,0:T(8,128)(2,1)} async-done(((bf16[256,1024]{1,0:T(8,128)(2,1)}), bf16[512,1024]{1,0:T(8,128)(2,1)}) %all-gather.8.cloned.1.call-update) | async-done | bytes 1048592 | tf_op jit(solution)/shard_map/all_gather | solution.py:59
  34.7 71.8 %all-gather.10.cloned.1.call-done = bf16[1024,1536]{1,0:T(8,128)(2,1)} async-done(((bf16[64,1536]{1,0:T(8,128)(2,1)}), bf16[1024,1536]{1,0:T(8,128)(2,1)}) %all-gather.10.cloned.1.call-update) | async-done | bytes 3145744 | tf_op jit(solution)/shard_map/all_gather | solution.py:219
  106.5 3.2 fusion.15
  109.6 1.3 copy-done.13
  112.5 1.3 slice.106
  115.4 1.5 fusion.7
  116.9 1.8 exponential_reduce_fusion
  118.7 2.3 convolution_convert_fusion.7
  121.0 2.2 fusion.37
  123.2 1.3 copy-done.3
  124.6 1.5 collective-permute-start
  126.2 12.7 %collective-permute-done = bf16[256,1024]{1,0:T(8,128)(2,1)} collective-permute-done((bf16[256,1024]{1,0:T(8,128)(2,1)S(1)}, bf16[256,1024]{1,0:T(8,128)(2,1)}, u32[]{:S(2)}, u32[]{:S(2)}) %collective-permute-start) | collective-permute-done | bytes 524320 | tf_op jit(solution)/shard_map/ppermute | solution.py:70
  138.9 1.7 multiply_reduce_fusion.2
  143.6 1.5 bitcast_compare_fusion
  145.1 16.8 %all-gather.12.cloned.1.call-done = bf16[512,1024]{1,0:T(8,128)(2,1)} async-done(((bf16[256,1024]{1,0:T(8,128)(2,1)}), bf16[512,1024]{1,0:T(8,128)(2,1)}) %all-gather.12.cloned.1.call-update) | async-done | bytes 1048592 | tf_op jit(solution)/shard_map/all_gather | solution.py:59
  162.0 5.8 convolution_convert_fusion
  167.8 6.0 all-to-all-start
  173.8 3.6 fusion.55
  177.4 92.3 %all-to-all-done = bf16[16,160,1024]{2,1,0:T(8,128)(2,1)} async-done(((bf16[16,160,1024]{2,1,0:T(8,128)(2,1)}), bf16[16,160,1024]{2,1,0:T(8,128)(2,1)}, u32[]{:S(2)}, u32[]{:S(2)}) %all-to-all-start) | async-done | bytes 5242912 | tf_op jit(solution)/shard_map/all_to_all | solution.py:237
  269.7 5.2 fusion.60
  274.9 9.8 %multiply_convert_fusion.3 = (bf16[2560,512]{1,0:T(8,128)(2,1)S(1)}, f32[2560,512]{1,0:T(8,128)}) fusion(f32[2560,512]{1,0:T(8,128)S(1)} %fusion.60, bf16[2560,1024]{1,0:T(8,128)(2,1)} %bitcast.16, bf16[1024,512]{1,0:T(8,128)(2,1)S(1)} %bitcast.187), kind=kOutput, calls=%fused_computation.21 | convolution fusion | flops 2692218880 | bytes 19398656 | tf_op jit(solution)/shard_map/ecd,edf->ecf/dot_general | solution.py:291
  284.8 4.9 convolution_convert_fusion.1
  289.7 23.9 %all-to-all-start.2 = ((bf16[16,160,1024]{2,1,0:T(8,128)(2,1)}), bf16[16,160,1024]{2,1,0:T(8,128)(2,1)}, u32[]{:S(2)}, u32[]{:S(2)}) async-start(bf16[16,160,1024]{2,1,0:T(8,128)(2,1)} %bitcast.173), calls=%async_computation.2 | async-start | bytes 10485760 | tf_op jit(solution)/shard_map/all_to_all | solution.py:245
  314.1 1.5 fusion.42
  315.6 21.7 %all-gather.14.cloned.1.call-done = bf16[512,1024]{1,0:T(8,128)(2,1)} async-done(((bf16[256,1024]{1,0:T(8,128)(2,1)}), bf16[512,1024]{1,0:T(8,128)(2,1)}) %all-gather.14.cloned.1.call-update) | async-done | bytes 1048592 | tf_op jit(solution)/shard_map/all_gather | solution.py:59
  337.3 72.2 %all-to-all-done.2 = bf16[16,160,1024]{2,1,0:T(8,128)(2,1)} async-done(((bf16[16,160,1024]{2,1,0:T(8,128)(2,1)}), bf16[16,160,1024]{2,1,0:T(8,128)(2,1)}, u32[]{:S(2)}, u32[]{:S(2)}) %all-to-all-start.2) | async-done | bytes 5242912 | tf_op jit(solution)/shard_map/all_to_all | solution.py:245
  409.5 8.3 fusion
  418.6 3.4 select_reduce_fusion.1
  422.1 4.6 multiply_convert_fusion
  426.7 138.5 %all_to_all.30 = bf16[16,160,1024]{2,1,0:T(8,128)(2,1)S(1)} all-to-all(bf16[16,160,1024]{2,1,0:T(8,128)(2,1)S(1)} %bitcast.168), channel_id=1, replica_groups=mesh['dp'=16,'tensor'=2] {'dp'}, dimensions={0} | all-to-all | bytes 10485760 | tf_op jit(solution)/shard_map/all_to_all | solution.py:237
  565.2 9.0 multiply_convert_fusion.1
  574.3 2.9 fusion.61
  577.3 4.8 add_convert_fusion
  582.1 5.6 all-to-all-start.4
  587.9 4.9 fusion.17
  592.8 1.3 copy-done.14
  595.5 88.1 %all-to-all-done.4 = bf16[16,160,1024]{2,1,0:T(8,128)(2,1)} async-done(((bf16[16,160,1024]{2,1,0:T(8,128)(2,1)}), bf16[16,160,1024]{2,1,0:T(8,128)(2,1)}, u32[]{:S(2)}, u32[]{:S(2)}) %all-to-all-start.4) | async-done | bytes 5242912 | tf_op jit(solution)/shard_map/all_to_all | solution.py:245
  683.6 5.1 fusion.18
  689.4 6.5 convolution_convert_fusion.3
  696.0 7.5 collective-permute-done.2
  704.5 2.9 fusion.54
  707.4 6.3 convolution_convert_fusion.4
  713.7 5.5 convolution_convert_fusion.5
  719.3 2.0 maximum_bitcast_fusion
  721.3 23.9 %all-to-all-start.5 = ((bf16[16,3,64,512]{3,2,1,0:T(8,128)(2,1)}), bf16[16,3,64,512]{3,2,1,0:T(8,128)(2,1)}, u32[]{:S(2)}, u32[]{:S(2)}) async-start(bf16[16,3,64,512]{3,2,1,0:T(8,128)(2,1)} %maximum_bitcast_fusion), calls=%async_computation.6 | async-start | bytes 6291456 | tf_op jit(solution)/shard_map/all_to_all | solution.py:328
  746.6 2.3 convolution_convert_fusion.8
  748.9 5.3 fusion.1
  754.8 2.7 fusion.3
  757.5 1.4 broadcast_multiply_fusion
  761.9 2.2 fusion.23
  764.9 1.3 convolution_convert_fusion.2
  766.5 3.0 copy.98
  769.9 3.1 fusion.13
  773.0 1.3 copy-done.6
  775.5 34.4 %all-to-all-done.5 = bf16[16,3,64,512]{3,2,1,0:T(8,128)(2,1)} async-done(((bf16[16,3,64,512]{3,2,1,0:T(8,128)(2,1)}), bf16[16,3,64,512]{3,2,1,0:T(8,128)(2,1)}, u32[]{:S(2)}, u32[]{:S(2)}) %all-to-all-start.5) | async-done | bytes 3145760 | tf_op jit(solution)/shard_map/all_to_all | solution.py:328
  810.0 2.7 convert_element_type.229
  812.8 3.3 slice_bitcast_fusion
  816.7 85.9 %all-gather.1 = f32[32,2,1024]{2,1,0:T(2,128)S(1)} all-gather(f32[1,2,1024]{2,1,0:T(2,128)S(1)} %maximum_bitcast_fusion.1), channel_id=2, replica_groups=mesh['dp'=16,'tensor'=2] {'dp','tensor'}, dimensions={0}, use_global_device_ids=true | all-gather | bytes 270336 | tf_op jit(solution)/shard_map/all_gather | solution.py:375
  903.3 2.5 fusion.29
  (184 shorter events, 24.6 us)
Async XLA Ops:
  7.2 27.5 %all-gather.8.cloned.1.call-start = ((), (), s32[]{:S(2)}) async-start(), calls=%async_computation.8 | async-start | bytes 1572864 | tf_op jit(solution)/shard_map/all_gather | solution.py:59
  8.5 7.6 copy-start.38
  10.5 95.9 %all-gather.10.cloned.1.call-start = ((), (), s32[]{:S(2)}) async-start(), calls=%async_computation.9 | async-start | bytes 3342336 | tf_op jit(solution)/shard_map/all_gather | solution.py:219
  16.1 151.7 %all-to-all-start.1 = ((bf16[16,3,64,512]{3,2,1,0:T(8,128)(2,1)}), bf16[16,3,64,512]{3,2,1,0:T(8,128)(2,1)}, u32[]{:S(2)}, u32[]{:S(2)}) async-start(bf16[16,3,64,512]{3,2,1,0:T(8,128)(2,1)} %pad_maximum_fusion), calls=%async_computation.1 | async-start | bytes 6291456 | tf_op jit(solution)/shard_map/all_to_all | solution.py:226
  23.5 138.5 %all-gather.12.cloned.1.call-start = ((), (), s32[]{:S(2)}) async-start(), calls=%async_computation.10 | async-start | bytes 1572864 | tf_op jit(solution)/shard_map/all_gather | solution.py:59
  23.9 91.2 %copy-start.8 = (f32[512,64]{0,1:T(8,128)}, f32[512,64]{0,1:T(8,128)S(1)}, u32[]{:S(2)}) copy-start(f32[512,64]{0,1:T(8,128)S(1)} %pad_maximum_fusion.7) | copy-start | bytes 393220
  109.6 1.3 copy-start.13
  116.8 4.2 copy-start
  116.8 1.8 copy-start.11
  118.6 20.2 %copy-start.1 = (bf16[256,1024]{1,0:T(8,128)(2,1)S(1)}, bf16[256,1024]{1,0:T(8,128)(2,1)}, u32[]{:S(2)}) copy-start(bf16[256,1024]{1,0:T(8,128)(2,1)} %param.13) | copy-start | bytes 1572868
  121.0 21.4 %copy-start.22 = (bf16[4,64,2,512]{3,1,2,0:T(8,128)(2,1)}, bf16[4,64,2,512]{3,1,2,0:T(8,128)(2,1)S(1)}, u32[]{:S(2)}) copy-start(bf16[4,64,2,512]{3,1,2,0:T(8,128)(2,1)S(1)} %convolution_convert_fusion.7) | copy-start | bytes 1572868
  121.0 19.6 %copy-start.34 = (f32[1024]{0:T(1024)S(1)}, f32[1024]{0:T(1024)}, u32[]{:S(2)}) copy-start(f32[1024]{0:T(1024)} %param.15) | copy-start | bytes 12292
  121.0 21.2 %copy-start.27 = (s32[512,8]{0,1:T(8,128)S(1)}, s32[512,8]{0,1:T(8,128)}, u32[]{:S(2)}) copy-start(s32[512,8]{0,1:T(8,128)} %param.24) | copy-start | bytes 49156
  123.2 1.3 copy-start.3
  124.6 14.3 %collective-permute-start = (bf16[256,1024]{1,0:T(8,128)(2,1)S(1)}, bf16[256,1024]{1,0:T(8,128)(2,1)}, u32[]{:S(2)}, u32[]{:S(2)}) collective-permute-start(bf16[256,1024]{1,0:T(8,128)(2,1)S(1)} %dynamic-slice_convert_fusion.3), channel_id=1, source_target_pairs={{0,1},{1,0},{2,3},{3,2},{4,5},{5,4},{6,7},{7,6},{8,9},{9,8},{10,11... | collective-permute-start | bytes 1572872 | tf_op jit(solution)/shard_map/ppermute | solution.py:70
  167.8 101.9 %all-to-all-start = ((bf16[16,160,1024]{2,1,0:T(8,128)(2,1)}), bf16[16,160,1024]{2,1,0:T(8,128)(2,1)}, u32[]{:S(2)}, u32[]{:S(2)}) async-start(bf16[16,160,1024]{2,1,0:T(8,128)(2,1)} %bitcast.175), calls=%async_computation | async-start | bytes 10485760 | tf_op jit(solution)/shard_map/all_to_all | solution.py:237
  269.7 5.2 copy-start.16
  274.9 9.9 %copy-start.51 = (f32[2560,512]{1,0:T(8,128)}, f32[2560,512]{1,0:T(8,128)S(1)}, u32[]{:S(2)}) copy-start(f32[2560,512]{1,0:T(8,128)S(1)} %fusion.60) | copy-start | bytes 15728644
  274.9 9.8 %copy-start.19 = (bf16[16,1,64,512]{3,2,1,0:T(8,128)(2,1)S(1)}, bf16[16,1,64,512]{3,2,1,0:T(8,128)(2,1)}, u32[]{:S(2)}) copy-start(bf16[16,1,64,512]{3,2,1,0:T(8,128)(2,1)} %get-tuple-element.120) | copy-start | bytes 3145732
  284.8 4.9 copy-start.48
  289.7 119.8 %all-to-all-start.2 = ((bf16[16,160,1024]{2,1,0:T(8,128)(2,1)}), bf16[16,160,1024]{2,1,0:T(8,128)(2,1)}, u32[]{:S(2)}, u32[]{:S(2)}) async-start(bf16[16,160,1024]{2,1,0:T(8,128)(2,1)} %bitcast.173), calls=%async_computation.2 | async-start | bytes 10485760 | tf_op jit(solution)/shard_map/all_to_all | solution.py:245
  313.6 23.8 %all-gather.14.cloned.1.call-start = ((), (), s32[]{:S(2)}) async-start(), calls=%async_computation.11 | async-start | bytes 1572864 | tf_op jit(solution)/shard_map/all_gather | solution.py:59
  426.7 138.5 %copy-start.20 = (bf16[16,1,64,512]{3,2,1,0:T(8,128)(2,1)S(1)}, bf16[16,1,64,512]{3,2,1,0:T(8,128)(2,1)}, u32[]{:S(2)}) copy-start(bf16[16,1,64,512]{3,2,1,0:T(8,128)(2,1)} %get-tuple-element.120) | copy-start | bytes 3145732
  565.2 9.1 copy-start.4
  565.2 9.1 copy-start.18
  574.3 3.0 copy-start.46
  574.3 3.0 copy-start.50
  574.3 3.0 copy-start.17
  582.1 5.8 copy-start.30
  582.1 5.8 copy-start.32
  582.1 101.5 %all-to-all-start.4 = ((bf16[16,160,1024]{2,1,0:T(8,128)(2,1)}), bf16[16,160,1024]{2,1,0:T(8,128)(2,1)}, u32[]{:S(2)}, u32[]{:S(2)}) async-start(bf16[16,160,1024]{2,1,0:T(8,128)(2,1)} %bitcast.174), calls=%async_computation.4 | async-start | bytes 10485760 | tf_op jit(solution)/shard_map/all_to_all | solution.py:245
  587.7 158.9 %all-gather.16.cloned.1.call-start = ((), (), s32[]{:S(2)}) async-start(), calls=%async_computation.12 | async-start | bytes 1572864 | tf_op jit(solution)/shard_map/all_gather | solution.py:59
  592.8 1.3 copy-start.14
  595.0 109.5 %collective-permute-start.1 = (bf16[256,1024]{1,0:T(8,128)(2,1)}, bf16[256,1024]{1,0:T(8,128)(2,1)}, u32[]{:S(2)}, u32[]{:S(2)}) collective-permute-start(bf16[256,1024]{1,0:T(8,128)(2,1)} %dynamic-slice_convert_fusion.2), channel_id=1, source_target_pairs={{0,1},{1,0},{2,3},{3,2},{4,5},{5,4},{6,7},{7,6},{8,9},{9,8},{10,11... | collective-permute-start | bytes 1572872 | tf_op jit(solution)/shard_map/ppermute | solution.py:70
  683.6 5.8 copy-start.49
  688.7 14.8 %copy-start.35 = (f32[1024]{0:T(1024)S(1)}, f32[1024]{0:T(1024)}, u32[]{:S(2)}) copy-start(f32[1024]{0:T(1024)} %param.15) | copy-start | bytes 12292
  688.7 14.8 %copy-start.37 = (f32[256]{0:T(256)S(1)}, f32[256]{0:T(256)}, u32[]{:S(2)}) copy-start(f32[256]{0:T(256)} %copy-done.36) | copy-start | bytes 3076
  688.8 15.7 %copy-start.10 = (bf16[256,1024]{1,0:T(8,128)(2,1)S(1)}, bf16[256,1024]{1,0:T(8,128)(2,1)}, u32[]{:S(2)}) copy-start(bf16[256,1024]{1,0:T(8,128)(2,1)} %param.25) | copy-start | bytes 1572868
  688.8 15.7 %copy-start.15 = (f32[512,1024]{1,0:T(8,128)S(1)}, f32[512,1024]{1,0:T(8,128)}, u32[]{:S(2)}) copy-start(f32[512,1024]{1,0:T(8,128)} %copy-done.14) | copy-start | bytes 6291460
  688.8 14.7 %collective-permute-start.2 = (bf16[256,1024]{1,0:T(8,128)(2,1)S(1)}, bf16[256,1024]{1,0:T(8,128)(2,1)S(1)}, u32[]{:S(2)}, u32[]{:S(2)}) collective-permute-start(bf16[256,1024]{1,0:T(8,128)(2,1)S(1)} %dynamic-slice_convert_fusion.1), channel_id=1, source_target_pairs={{0,1},{1,0},{2,3},{3,2},{4,5},{5,4},{6,7},{7,6},{8,9},{9,8},{10,11... | collective-permute-start | bytes 1572872 | tf_op jit(solution)/shard_map/ppermute | solution.py:70
  707.4 6.4 copy-start.47
  713.7 5.5 copy-start.21
  721.3 27.6 %copy-start.12 = (bf16[512,256]{0,1:T(8,128)(2,1)S(1)}, bf16[512,256]{0,1:T(8,128)(2,1)}, u32[]{:S(2)}) copy-start(bf16[512,256]{0,1:T(8,128)(2,1)} %copy.75) | copy-start | bytes 786436
  721.3 88.7 %all-to-all-start.5 = ((bf16[16,3,64,512]{3,2,1,0:T(8,128)(2,1)}), bf16[16,3,64,512]{3,2,1,0:T(8,128)(2,1)}, u32[]{:S(2)}, u32[]{:S(2)}) async-start(bf16[16,3,64,512]{3,2,1,0:T(8,128)(2,1)} %maximum_bitcast_fusion), calls=%async_computation.6 | async-start | bytes 6291456 | tf_op jit(solution)/shard_map/all_to_all | solution.py:328
  745.1 160.7 %reduce-scatter.7.cloned.1.call-start = ((), (), s32[]{:S(2)}) async-start(), calls=%async_computation.14 | async-start | bytes 3342336
  748.9 5.3 slice-start
  748.9 5.9 slice-start.1
  758.9 1.3 copy-start.9
  759.8 1.4 copy-start.44
  760.5 3.7 copy-start.24
  761.2 3.0 copy-start.25
  761.9 3.0 copy-start.43
  766.5 3.4 copy-start.26
  769.5 5.2 copy-start.28
  769.5 5.2 copy-start.29
  769.6 5.2 copy-start.42
  769.6 140.6 %reduce-scatter.5.cloned.1.call-start = ((), (), s32[]{:S(2)}) async-start(), calls=%async_computation.13 | async-start | bytes 24576 | tf_op jit(solution)/shard_map/reduce_scatter | solution.py:350
  774.4 41.7 %collective-permute-start.3 = (bf16[256,1024]{1,0:T(8,128)(2,1)S(1)}, bf16[256,1024]{1,0:T(8,128)(2,1)S(1)}, u32[]{:S(2)}, u32[]{:S(2)}) collective-permute-start(bf16[256,1024]{1,0:T(8,128)(2,1)S(1)} %dynamic-slice_convert_fusion), channel_id=1, source_target_pairs={{0,1},{1,0},{2,3},{3,2},{4,5},{5,4},{6,7},{7,6},{8,9},{9,8},{10,11... | collective-permute-start | bytes 1572872 | tf_op jit(solution)/shard_map/ppermute | solution.py:70
  812.7 3.4 copy-start.2
  812.7 3.4 copy-start.7
  812.7 3.4 copy-start.33
  812.7 3.4 copy-start.39
  812.7 3.9 copy-start.40
  812.8 90.6 %copy-start.5 = (f32[256,1024]{1,0:T(8,128)S(1)}, f32[256,1024]{1,0:T(8,128)}, u32[]{:S(2)}) copy-start(f32[256,1024]{1,0:T(8,128)} %get-tuple-element.112) | copy-start | bytes 3145732
  (6 other events, 5.2 us)
Sparse Core Ops, SparseCore 0:
  10.6 23.9 all-gather.7
  37.5 68.8 all-gather.9
  141.7 20.2 all-gather.11
  315.6 21.6 all-gather.13
  707.5 39.0 all-gather.15
  769.6 74.3 reduce-scatter.6
  846.8 8.6 reduce-scatter.4

commit v2 on v1

--- a/solution.py
+++ b/solution.py
@@ -214,23 +214,13 @@
     key_width = w_key.shape[1]
     pre_width = query_width + 2 * key_width
     rows_shard = w_query.shape[0]
-    owns_experts = local_experts == lax.axis_size("dp")
+    owns_experts = local_experts == lax.axis_size("dp") and 2 * w_gate.shape[2] == D
     cosine, sine_table = rope_tables(group_rows, seq_length)
     attn_full = lax.all_gather(
         jnp.concatenate([w_query, w_key, w_value, w_out.T], 1), "dp", axis=0, tiled=True
     )
     pre_full = attn_full[:, :pre_width]
     out_full = attn_full[:, pre_width:]
-    expert_stack = jnp.stack([w_gate, w_up, w_down.transpose(0, 2, 1)], 1)
-    if owns_experts:
-        expert_full = lax.all_to_all(expert_stack, "dp", split_axis=0, concat_axis=0, tiled=True)
-        gate_full, up_full, down_full = (
-            expert_full[:, index].reshape(1, D, expert_stack.shape[3]) for index in range(3)
-        )
-    else:
-        expert_full = lax.all_gather(expert_stack, "dp", axis=2, tiled=True)
-        gate_full, up_full, down_full = (expert_full[:, index] for index in range(3))
-
     def to_experts(rows):
         if not owns_experts:
             return rows.reshape(local_experts, capacity, D)
@@ -257,7 +247,38 @@
     slot_gate = jnp.sum(jnp.where(slots, row_gates[:, :, None], 0.0), 0).reshape(-1)
     grad_full = spread(cotangent)
     grad_slots = jnp.einsum("ts,td->sd", slot_rows, grad_full, preferred_element_type=jnp.float32)
-    grad_expert = to_experts((slot_gate[:, None] * grad_slots).astype(jnp.bfloat16))
+    grad_rows = (slot_gate[:, None] * grad_slots).astype(jnp.bfloat16)
+    down_rows = w_down.transpose(0, 2, 1)
+    if owns_experts:
+        half = rows_shard // 2
+        width = w_gate.shape[2]
+        moved = lax.all_to_all(
+            jnp.concatenate(
+                [
+                    jnp.concatenate([w_gate, w_up], 2),
+                    jnp.concatenate([down_rows[:, :half], down_rows[:, half:]], 2),
+                    grad_rows.reshape(local_experts, capacity, D),
+                ],
+                1,
+            ),
+            "dp",
+            split_axis=0,
+            concat_axis=0,
+            tiled=True,
+        )
+        gate_full = moved[:, :rows_shard, :width].reshape(1, D, width)
+        up_full = moved[:, :rows_shard, width:].reshape(1, D, width)
+        down_moved = moved[:, rows_shard : rows_shard + half]
+        down_full = jnp.concatenate(
+            [down_moved[:, :, :width], down_moved[:, :, width:]], 1
+        ).reshape(1, D, width)
+        grad_expert = moved[:, rows_shard + half :].reshape(1, local_experts * capacity, D)
+    else:
+        expert_full = lax.all_gather(
+            jnp.stack([w_gate, w_up, down_rows], 1), "dp", axis=2, tiled=True
+        )
+        gate_full, up_full, down_full = (expert_full[:, index] for index in range(3))
+        grad_expert = to_experts(grad_rows)
 
     token_values = tokens.astype(jnp.float32)
     normed_own, scaled_attn, factor_attn = normalize(token_values, gain_attn)
@@ -377,14 +398,16 @@
     )
     gain_sums = jnp.sum(gain_parts, 0)
     grad_gain_attn, grad_gain_ffn = (gain_sums[0], gain_sums[1])
-    attn_shards = lax.psum_scatter(
+    attn_moved = lax.all_to_all(
         jnp.concatenate(
             [grad_pre_w.astype(jnp.bfloat16), grad_out_w.astype(jnp.bfloat16)], 1
-        ),
+        ).reshape(-1, rows_shard, pre_width + query_width),
         "dp",
-        scatter_dimension=0,
+        split_axis=0,
+        concat_axis=0,
         tiled=True,
-    ).astype(jnp.float32)
+    )
+    attn_shards = jnp.sum(attn_moved.astype(jnp.float32), 0)
     grad_query = attn_shards[:, :query_width]
     grad_key = attn_shards[:, query_width : query_width + key_width]
     grad_value = attn_shards[:, query_width + key_width : pre_width]

time: 928 us -> 909 us (0.980)
  blocking collectives: 224 us -> 89.5 us
  waiting for transfers between devices: 430 us -> 518 us
  starting transfers between devices: 70.8 us -> 102 us
    all_to_all x1 -> x0, blocking collectives: 139 us -> none  [to_experts(): lax.all_to_all(rows.reshape(local_experts, capacity, D), 'dp', split_axis...]
    all_gather x1, waiting for transfers between devices: 71.8 us -> 122 us  [on_device(): lax.all_gather(jnp.concatenate([w_query, w_key, w_value, w_out.T], 1), 'd...]
    all_gather x4, waiting for transfers between devices: 50.4 us -> 84.1 us  [spread(): return lax.all_gather(values, 'tensor', axis=0, tiled=True)]
    all_to_all x2, starting transfers between devices: 29.4 us -> 47.8 us  [from_experts(): lax.all_to_all(rows.reshape(local_experts, capacity, D), 'dp', split_axis...]
    all_to_all x1 -> x2, starting transfers between devices: 7.4 us -> 21.3 us  [the longest x1 15.5 us: on_device(): lax.all_to_all(jnp.concatenate([grad_pre_w.astype(jnp.bfloat16), grad_out...]
    unnamed x114 -> x108, local copies, waits for them, and re-layouts: 15.4 us -> 4.87 us
  transfers between devices with their start and end apart: 16 -> 16, of which waited for: 11 -> 12; matrix products, arithmetic and copies ran while one was open for 12% -> 15% of each run, Pallas kernels for 0% -> 0%
where the time goes in v2:
time: 909 us; the launch traced here: 903 us
  waiting for transfers between devices  518 us (57%)
  starting transfers between devices  102 us (11%)
  matrix products  102 us (11%)
  blocking collectives  89.5 us (10%)
  other arithmetic  44.7 us (5%)
  local copies, waits for them, and re-layouts  31.7 us (3%)
  between operations  15.3 us (2%)
    all_to_all x2, waiting for transfers between devices, from_experts(): lax.all_to_all(rows.reshape(local_experts, capacity, D), 'dp', split_axis...  166 us
    all_gather x1, waiting for transfers between devices, on_device(): lax.all_gather(jnp.concatenate([w_query, w_key, w_value, w_out.T], 1), 'd...  122 us
    all_gather x1, blocking collectives, on_device(): lax.all_gather(jnp.stack([gain_attn_part, gain_ffn_part]), ('dp', 'tensor...  89.5 us
    all_to_all x1, waiting for transfers between devices, to_experts(): lax.all_to_all(rows.reshape(local_experts, capacity, D), 'dp', split_axis...  84.8 us
    all_gather x4, waiting for transfers between devices, spread(): return lax.all_gather(values, 'tensor', axis=0, tiled=True)  84.1 us
    all_to_all x2, starting transfers between devices, from_experts(): lax.all_to_all(rows.reshape(local_experts, capacity, D), 'dp', split_axis...  47.8 us
    all_to_all x1, waiting for transfers between devices, on_device(): lax.all_to_all(grad_stack.reshape(3, local_experts, rows_shard, -1).trans...  32.1 us
    ppermute x4, waiting for transfers between devices, sum_rows(): lax.ppermute(sent.astype(jnp.bfloat16), 'tensor', [(0, 1), (1, 0)])  27.1 us
  transfers between devices with their start and end apart: 16, of which 12 were waited for; matrix products, arithmetic and copies ran while one was open for 15% of the time, Pallas kernels for 0%

profile of v2, /device:TPU:0, one launch (start us, length us, event | category | flops | bytes accessed | tf_op | source)
XLA Modules:
  0.0 903.4 jit_solution(2138044452122655128)
XLA Ops:
  11.9 1.8 fusion.58
  13.6 20.0 %all-gather.14.cloned.1.call-done = bf16[512,1024]{1,0:T(8,128)(2,1)} async-done(((bf16[256,1024]{1,0:T(8,128)(2,1)}), bf16[512,1024]{1,0:T(8,128)(2,1)}) %all-gather.14.cloned.1.call-update) | async-done | bytes 1048592 | tf_op jit(solution)/shard_map/all_gather | solution.py:59
  33.6 6.9 multiply_convert_fusion
  40.6 3.8 pad_maximum_fusion
  44.4 5.8 all-to-all-start.1
  54.0 20.9 %all-gather.8.cloned.1.call-done = bf16[512,1024]{1,0:T(8,128)(2,1)} async-done(((bf16[256,1024]{1,0:T(8,128)(2,1)}), bf16[512,1024]{1,0:T(8,128)(2,1)}) %all-gather.8.cloned.1.call-update) | async-done | bytes 1048592 | tf_op jit(solution)/shard_map/all_gather | solution.py:59
  74.8 122.3 %all-gather.10.cloned.1.call-done = bf16[1024,1536]{1,0:T(8,128)(2,1)} async-done(((bf16[64,1536]{1,0:T(8,128)(2,1)}), bf16[1024,1536]{1,0:T(8,128)(2,1)}) %all-gather.10.cloned.1.call-update) | async-done | bytes 3145744 | tf_op jit(solution)/shard_map/all_gather | solution.py:219
  197.2 3.2 fusion.15
  206.2 1.5 fusion.7
  207.7 1.8 exponential_reduce_fusion
  209.5 2.3 convolution_convert_fusion.7
  211.8 3.3 fusion.37
  215.1 1.3 dynamic-slice_convert_fusion.3
  217.3 13.4 %collective-permute-done = bf16[256,1024]{1,0:T(8,128)(2,1)} collective-permute-done((bf16[256,1024]{1,0:T(8,128)(2,1)S(1)}, bf16[256,1024]{1,0:T(8,128)(2,1)}, u32[]{:S(2)}, u32[]{:S(2)}) %collective-permute-start) | collective-permute-done | bytes 524320 | tf_op jit(solution)/shard_map/ppermute | solution.py:70
  230.7 1.7 multiply_reduce_fusion.2
  232.4 1.6 multiply_convert_fusion.4
  234.0 37.6 %all-gather.12.cloned.1.call-done = bf16[512,1024]{1,0:T(8,128)(2,1)} async-done(((bf16[256,1024]{1,0:T(8,128)(2,1)}), bf16[512,1024]{1,0:T(8,128)(2,1)}) %all-gather.12.cloned.1.call-update) | async-done | bytes 1048592 | tf_op jit(solution)/shard_map/all_gather | solution.py:59
  271.6 7.0 convolution_convert_fusion
  278.6 5.7 all-to-all-start
  284.3 5.7 slice.135
  289.9 1.3 fusion.55
  292.3 3.1 fusion.56
  295.4 84.8 %all-to-all-done = bf16[16,160,1024]{2,1,0:T(8,128)(2,1)} async-done(((bf16[16,160,1024]{2,1,0:T(8,128)(2,1)}), bf16[16,160,1024]{2,1,0:T(8,128)(2,1)}, u32[]{:S(2)}, u32[]{:S(2)}) %all-to-all-start) | async-done | bytes 5242912 | tf_op jit(solution)/shard_map/all_to_all | solution.py:227
  380.2 5.3 fusion.63
  385.5 5.0 fusion.62
  390.6 7.0 multiply_convert_fusion.1
  397.6 4.8 convolution_convert_fusion.1
  402.4 23.9 %all-to-all-start.2 = ((bf16[16,160,1024]{2,1,0:T(8,128)(2,1)}), bf16[16,160,1024]{2,1,0:T(8,128)(2,1)}, u32[]{:S(2)}, u32[]{:S(2)}) async-start(bf16[16,160,1024]{2,1,0:T(8,128)(2,1)} %bitcast.175), calls=%async_computation.2 | async-start | bytes 10485760 | tf_op jit(solution)/shard_map/all_to_all | solution.py:235
  426.3 5.3 fusion.64
  431.6 5.1 add_convert_fusion
  436.7 85.6 %all-to-all-done.2 = bf16[16,160,1024]{2,1,0:T(8,128)(2,1)} async-done(((bf16[16,160,1024]{2,1,0:T(8,128)(2,1)}), bf16[16,160,1024]{2,1,0:T(8,128)(2,1)}, u32[]{:S(2)}, u32[]{:S(2)}) %all-to-all-start.2) | async-done | bytes 5242912 | tf_op jit(solution)/shard_map/all_to_all | solution.py:235
  522.2 23.9 %all-to-all-start.3 = ((bf16[16,160,1024]{2,1,0:T(8,128)(2,1)}), bf16[16,160,1024]{2,1,0:T(8,128)(2,1)}, u32[]{:S(2)}, u32[]{:S(2)}) async-start(bf16[16,160,1024]{2,1,0:T(8,128)(2,1)} %bitcast.174), calls=%async_computation.3 | async-start | bytes 10485760 | tf_op jit(solution)/shard_map/all_to_all | solution.py:235
  546.4 7.2 convolution_convert_fusion.3
  553.6 4.9 fusion.17
  558.5 1.3 copy-done.9
  561.3 80.8 %all-to-all-done.3 = bf16[16,160,1024]{2,1,0:T(8,128)(2,1)} async-done(((bf16[16,160,1024]{2,1,0:T(8,128)(2,1)}), bf16[16,160,1024]{2,1,0:T(8,128)(2,1)}, u32[]{:S(2)}, u32[]{:S(2)}) %all-to-all-start.3) | async-done | bytes 5242912 | tf_op jit(solution)/shard_map/all_to_all | solution.py:235
  642.1 5.1 fusion.18
  647.9 6.5 convolution_convert_fusion.4
  654.4 7.5 collective-permute-done.2
  662.9 2.9 fusion.54
  665.9 6.3 convolution_convert_fusion.5
  672.1 3.3 maximum_bitcast_fusion
  675.5 23.9 %all-to-all-start.5 = ((bf16[16,3,64,512]{3,2,1,0:T(8,128)(2,1)}), bf16[16,3,64,512]{3,2,1,0:T(8,128)(2,1)}, u32[]{:S(2)}, u32[]{:S(2)}) async-start(bf16[16,3,64,512]{3,2,1,0:T(8,128)(2,1)} %maximum_bitcast_fusion), calls=%async_computation.6 | async-start | bytes 6291456 | tf_op jit(solution)/shard_map/all_to_all | solution.py:349
  699.4 5.7 all-gather.16.cloned.1.call-done
  705.1 2.3 convolution_convert_fusion.8
  707.4 5.3 fusion.1
  713.3 2.7 fusion.3
  717.5 1.4 broadcast_multiply_fusion
  719.9 2.2 fusion.23
  722.1 1.3 convolution_convert_fusion.2
  723.7 3.0 copy.73
  726.7 32.1 %all-to-all-done.5 = bf16[16,3,64,512]{3,2,1,0:T(8,128)(2,1)} async-done(((bf16[16,3,64,512]{3,2,1,0:T(8,128)(2,1)}), bf16[16,3,64,512]{3,2,1,0:T(8,128)(2,1)}, u32[]{:S(2)}, u32[]{:S(2)}) %all-to-all-start.5) | async-done | bytes 3145760 | tf_op jit(solution)/shard_map/all_to_all | solution.py:349
  758.8 15.5 %all-to-all-start.4 = ((bf16[16,64,1536]{2,1,0:T(8,128)(2,1)}), bf16[16,64,1536]{2,1,0:T(8,128)(2,1)}, u32[]{:S(2)}, u32[]{:S(2)}) async-start(bf16[16,64,1536]{2,1,0:T(8,128)(2,1)} %bitcast.53), calls=%async_computation.5 | async-start | bytes 6291456 | tf_op jit(solution)/shard_map/all_to_all | solution.py:401
  774.5 2.7 convert_element_type.229
  777.3 3.3 slice_bitcast_fusion
  781.5 1.3 fusion.13
  784.5 1.2 slice-done.4
  785.8 3.7 fusion
  789.6 1.5 select_reduce_fusion.1
  791.9 6.2 collective-permute-done.3
  798.2 1.7 fusion.30
  799.9 89.5 %all-gather.1 = f32[32,2,1024]{2,1,0:T(2,128)S(1)} all-gather(f32[1,2,1024]{2,1,0:T(2,128)S(1)} %maximum_bitcast_fusion.1), channel_id=2, replica_groups=mesh['dp'=16,'tensor'=2] {'dp','tensor'}, dimensions={0}, use_global_device_ids=true | all-gather | bytes 270336 | tf_op jit(solution)/shard_map/all_gather | solution.py:396
  890.1 2.5 fusion.29
  892.6 2.4 convert_reduce_fusion
  (183 shorter events, 28.6 us)
Async XLA Ops:
  7.2 26.4 %all-gather.14.cloned.1.call-start = ((), (), s32[]{:S(2)}) async-start(), calls=%async_computation.10 | async-start | bytes 1572864 | tf_op jit(solution)/shard_map/all_gather | solution.py:59
  8.0 1.7 copy-start.40
  11.8 28.7 %copy-start.3 = (pred[512,2560]{0,1:T(32,128)(4,1)}, pred[512,2560]{0,1:T(32,128)(4,1)S(1)}, u32[]{:S(2)}) copy-start(pred[512,2560]{0,1:T(32,128)(4,1)S(1)} %bitcast_compare_fusion) | copy-start | bytes 3932164
  13.6 26.9 %copy-start.11 = (bf16[16,64,512]{2,1,0:T(8,128)(2,1)S(1)}, bf16[16,64,512]{2,1,0:T(8,128)(2,1)}, u32[]{:S(2)}) copy-start(bf16[16,64,512]{2,1,0:T(8,128)(2,1)} %param.21) | copy-start | bytes 3145732
  33.6 7.0 copy-start.12
  44.3 5.9 copy-start.1
  44.3 6.1 copy-start.30
  44.3 7.2 copy-start.28
  44.3 7.2 copy-start.29
  44.4 7.2 copy-start.33
  44.4 7.2 copy-start.34
  44.4 234.2 %all-to-all-start.1 = ((bf16[16,256,1024]{2,1,0:T(8,128)(2,1)}), bf16[16,256,1024]{2,1,0:T(8,128)(2,1)}, u32[]{:S(2)}, u32[]{:S(2)}) async-start(bf16[16,256,1024]{2,1,0:T(8,128)(2,1)} %pad_maximum_fusion), calls=%async_computation.1 | async-start | bytes 16777216 | tf_op jit(solution)/shard_map/all_to_all | solution.py:255
  50.2 24.6 %all-gather.8.cloned.1.call-start = ((), (), s32[]{:S(2)}) async-start(), calls=%async_computation.7 | async-start | bytes 1572864 | tf_op jit(solution)/shard_map/all_gather | solution.py:59
  50.5 150.8 %copy-start.37 = (f32[256]{0:T(256)}, f32[256]{0:T(256)S(1)}, u32[]{:S(2)}) copy-start(f32[256]{0:T(256)S(1)} %add_rsqrt_fusion.1) | copy-start | bytes 3076
  51.5 145.7 %all-gather.10.cloned.1.call-start = ((), (), s32[]{:S(2)}) async-start(), calls=%async_computation.8 | async-start | bytes 3342336 | tf_op jit(solution)/shard_map/all_gather | solution.py:219
  52.3 219.3 %all-gather.12.cloned.1.call-start = ((), (), s32[]{:S(2)}) async-start(), calls=%async_computation.9 | async-start | bytes 1572864 | tf_op jit(solution)/shard_map/all_gather | solution.py:59
  207.7 4.2 copy-start
  207.7 1.8 copy-start.8
  216.4 14.2 %collective-permute-start = (bf16[256,1024]{1,0:T(8,128)(2,1)S(1)}, bf16[256,1024]{1,0:T(8,128)(2,1)}, u32[]{:S(2)}, u32[]{:S(2)}) collective-permute-start(bf16[256,1024]{1,0:T(8,128)(2,1)S(1)} %dynamic-slice_convert_fusion.3), channel_id=1, source_target_pairs={{0,1},{1,0},{2,3},{3,2},{4,5},{5,4},{6,7},{7,6},{8,9},{9,8},{10,11... | collective-permute-start | bytes 1572872 | tf_op jit(solution)/shard_map/ppermute | solution.py:70
  232.4 46.2 %copy-start.35 = (f32[256]{0:T(256)}, f32[256]{0:T(256)S(1)}, u32[]{:S(2)}) copy-start(f32[256]{0:T(256)S(1)} %add_rsqrt_fusion) | copy-start | bytes 3076
  278.6 101.6 %all-to-all-start = ((bf16[16,160,1024]{2,1,0:T(8,128)(2,1)}), bf16[16,160,1024]{2,1,0:T(8,128)(2,1)}, u32[]{:S(2)}, u32[]{:S(2)}) async-start(bf16[16,160,1024]{2,1,0:T(8,128)(2,1)} %bitcast.173), calls=%async_computation | async-start | bytes 10485760 | tf_op jit(solution)/shard_map/all_to_all | solution.py:227
  380.2 5.3 copy-start.16
  380.2 10.3 %slice-start.5 = ((s8[5242880]{0:T(1024)(128)(4,1)}), s8[4194304]{0:T(1024)(128)(4,1)S(1)}, s32[]{:S(2)}) async-start(s8[5242880]{0:T(1024)(128)(4,1)} %bitcast.170), calls=%async_computation.18 | async-start | bytes 8388608
  385.5 5.1 slice-start.6
  385.5 5.1 copy-start.13
  397.6 4.8 copy-start.46
  402.4 119.8 %all-to-all-start.2 = ((bf16[16,160,1024]{2,1,0:T(8,128)(2,1)}), bf16[16,160,1024]{2,1,0:T(8,128)(2,1)}, u32[]{:S(2)}, u32[]{:S(2)}) async-start(bf16[16,160,1024]{2,1,0:T(8,128)(2,1)} %bitcast.175), calls=%async_computation.2 | async-start | bytes 10485760 | tf_op jit(solution)/shard_map/all_to_all | solution.py:235
  426.3 5.3 copy-start.15
  426.3 5.3 copy-start.44
  522.2 119.8 %all-to-all-start.3 = ((bf16[16,160,1024]{2,1,0:T(8,128)(2,1)}), bf16[16,160,1024]{2,1,0:T(8,128)(2,1)}, u32[]{:S(2)}, u32[]{:S(2)}) async-start(bf16[16,160,1024]{2,1,0:T(8,128)(2,1)} %bitcast.174), calls=%async_computation.3 | async-start | bytes 10485760 | tf_op jit(solution)/shard_map/all_to_all | solution.py:235
  546.2 7.5 copy-start.21
  546.2 7.5 copy-start.27
  546.2 158.9 %all-gather.16.cloned.1.call-start = ((), (), s32[]{:S(2)}) async-start(), calls=%async_computation.11 | async-start | bytes 1572864 | tf_op jit(solution)/shard_map/all_gather | solution.py:59
  560.7 102.2 %collective-permute-start.1 = (bf16[256,1024]{1,0:T(8,128)(2,1)}, bf16[256,1024]{1,0:T(8,128)(2,1)}, u32[]{:S(2)}, u32[]{:S(2)}) collective-permute-start(bf16[256,1024]{1,0:T(8,128)(2,1)} %dynamic-slice_convert_fusion.2), channel_id=1, source_target_pairs={{0,1},{1,0},{2,3},{3,2},{4,5},{5,4},{6,7},{7,6},{8,9},{9,8},{10,11... | collective-permute-start | bytes 1572872 | tf_op jit(solution)/shard_map/ppermute | solution.py:70
  642.1 5.8 copy-start.45
  647.2 14.8 %copy-start.32 = (f32[1024]{0:T(1024)S(1)}, f32[1024]{0:T(1024)}, u32[]{:S(2)}) copy-start(f32[1024]{0:T(1024)} %param.15) | copy-start | bytes 12292
  647.2 14.8 %copy-start.36 = (f32[256]{0:T(256)S(1)}, f32[256]{0:T(256)}, u32[]{:S(2)}) copy-start(f32[256]{0:T(256)} %copy-done.35) | copy-start | bytes 3076
  647.3 15.7 %copy-start.7 = (bf16[256,1024]{1,0:T(8,128)(2,1)S(1)}, bf16[256,1024]{1,0:T(8,128)(2,1)}, u32[]{:S(2)}) copy-start(bf16[256,1024]{1,0:T(8,128)(2,1)} %param.25) | copy-start | bytes 1572868
  647.3 15.7 %copy-start.10 = (f32[512,1024]{1,0:T(8,128)S(1)}, f32[512,1024]{1,0:T(8,128)}, u32[]{:S(2)}) copy-start(f32[512,1024]{1,0:T(8,128)} %copy-done.9) | copy-start | bytes 6291460
  647.3 14.7 %collective-permute-start.2 = (bf16[256,1024]{1,0:T(8,128)(2,1)S(1)}, bf16[256,1024]{1,0:T(8,128)(2,1)S(1)}, u32[]{:S(2)}, u32[]{:S(2)}) collective-permute-start(bf16[256,1024]{1,0:T(8,128)(2,1)S(1)} %dynamic-slice_convert_fusion.1), channel_id=1, source_target_pairs={{0,1},{1,0},{2,3},{3,2},{4,5},{5,4},{6,7},{7,6},{8,9},{9,8},{10,11... | collective-permute-start | bytes 1572872 | tf_op jit(solution)/shard_map/ppermute | solution.py:70
  665.8 6.3 copy-start.14
  675.5 83.3 %all-to-all-start.5 = ((bf16[16,3,64,512]{3,2,1,0:T(8,128)(2,1)}), bf16[16,3,64,512]{3,2,1,0:T(8,128)(2,1)}, u32[]{:S(2)}, u32[]{:S(2)}) async-start(bf16[16,3,64,512]{3,2,1,0:T(8,128)(2,1)} %maximum_bitcast_fusion), calls=%async_computation.6 | async-start | bytes 6291456 | tf_op jit(solution)/shard_map/all_to_all | solution.py:349
  707.4 5.3 slice-start
  707.4 5.9 slice-start.1
  717.5 4.6 copy-start.17
  719.1 3.0 copy-start.23
  719.8 2.3 copy-start.42
  758.8 133.8 %all-to-all-start.4 = ((bf16[16,64,1536]{2,1,0:T(8,128)(2,1)}), bf16[16,64,1536]{2,1,0:T(8,128)(2,1)}, u32[]{:S(2)}, u32[]{:S(2)}) async-start(bf16[16,64,1536]{2,1,0:T(8,128)(2,1)} %bitcast.53), calls=%async_computation.5 | async-start | bytes 6291456 | tf_op jit(solution)/shard_map/all_to_all | solution.py:401
  774.3 122.1 %reduce-scatter.2.cloned.1.call-start = ((), (), s32[]{:S(2)}) async-start(), calls=%async_computation.12 | async-start | bytes 24576 | tf_op jit(solution)/shard_map/reduce_scatter | solution.py:371
  777.2 3.4 copy-start.18
  777.2 4.2 copy-start.19
  777.3 4.3 copy-start.24
  777.3 7.1 slice-start.2
  777.3 7.2 slice-start.3
  781.5 4.3 slice-start.4
  783.7 14.4 %collective-permute-start.3 = (bf16[256,1024]{1,0:T(8,128)(2,1)}, bf16[256,1024]{1,0:T(8,128)(2,1)S(1)}, u32[]{:S(2)}, u32[]{:S(2)}) collective-permute-start(bf16[256,1024]{1,0:T(8,128)(2,1)} %dynamic-slice_convert_fusion), channel_id=1, source_target_pairs={{0,1},{1,0},{2,3},{3,2},{4,5},{5,4},{6,7},{7,6},{8,9},{9,8},{10,11... | collective-permute-start | bytes 1572872 | tf_op jit(solution)/shard_map/ppermute | solution.py:70
  785.8 3.8 copy-start.22
  785.8 5.4 copy-start.25
  785.8 5.4 copy-start.41
  785.8 12.4 %copy-start.2 = (bf16[256,1024]{1,0:T(8,128)(2,1)S(1)}, bf16[256,1024]{1,0:T(8,128)(2,1)}, u32[]{:S(2)}) copy-start(bf16[256,1024]{1,0:T(8,128)(2,1)} %param.13) | copy-start | bytes 1572868
  785.8 12.4 %copy-start.31 = (f32[1024]{0:T(1024)S(1)}, f32[1024]{0:T(1024)}, u32[]{:S(2)}) copy-start(f32[1024]{0:T(1024)} %param.14) | copy-start | bytes 12292
  785.8 12.4 %copy-start.38 = (f32[256]{0:T(256)S(1)}, f32[256]{0:T(256)}, u32[]{:S(2)}) copy-start(f32[256]{0:T(256)} %copy-done.37) | copy-start | bytes 3076
  785.8 14.1 %copy-start.39 = (f32[1024]{0:T(1024)S(1)}, f32[1024]{0:T(1024)}, u32[]{:S(2)}) copy-start(f32[1024]{0:T(1024)} %get-tuple-element.48) | copy-start | bytes 12292
  785.8 104.3 %copy-start.4 = (f32[256,1024]{1,0:T(8,128)S(1)}, f32[256,1024]{1,0:T(8,128)}, u32[]{:S(2)}) copy-start(f32[256,1024]{1,0:T(8,128)} %get-tuple-element.62) | copy-start | bytes 3145732
  (6 other events, 7.8 us)
Sparse Core Ops, SparseCore 0:
  9.6 23.9 all-gather.13
  53.2 21.6 all-gather.7
  77.7 119.4 all-gather.9
  234.2 37.4 all-gather.11
  666.0 39.0 all-gather.15
  792.0 10.0 reduce-scatter.1

commit v3 on v2

--- a/solution.py
+++ b/solution.py
@@ -219,8 +219,6 @@
     attn_full = lax.all_gather(
         jnp.concatenate([w_query, w_key, w_value, w_out.T], 1), "dp", axis=0, tiled=True
     )
-    pre_full = attn_full[:, :pre_width]
-    out_full = attn_full[:, pre_width:]
     def to_experts(rows):
         if not owns_experts:
             return rows.reshape(local_experts, capacity, D)
@@ -249,6 +247,12 @@
     grad_slots = jnp.einsum("ts,td->sd", slot_rows, grad_full, preferred_element_type=jnp.float32)
     grad_rows = (slot_gate[:, None] * grad_slots).astype(jnp.bfloat16)
     down_rows = w_down.transpose(0, 2, 1)
+    token_values = tokens.astype(jnp.float32)
+    normed_own, scaled_attn, factor_attn = normalize(token_values, gain_attn)
+    normed = spread(normed_own)
+    attn_full, normed, grad_rows = lax.optimization_barrier((attn_full, normed, grad_rows))
+    pre_full = attn_full[:, :pre_width]
+    out_full = attn_full[:, pre_width:]
     if owns_experts:
         half = rows_shard // 2
         width = w_gate.shape[2]
@@ -280,9 +284,6 @@
         gate_full, up_full, down_full = (expert_full[:, index] for index in range(3))
         grad_expert = to_experts(grad_rows)
 
-    token_values = tokens.astype(jnp.float32)
-    normed_own, scaled_attn, factor_attn = normalize(token_values, gain_attn)
-    normed = spread(normed_own)
     pre = jnp.dot(normed, pre_full, preferred_element_type=jnp.float32)
     query_pre = pre[:, :query_width]
     key_pre = pre[:, query_width : query_width + key_width]
@@ -313,11 +314,9 @@
     sigmoid_gate = jax.nn.sigmoid(gate_pre)
     silu_gate = gate_pre * sigmoid_gate
     hidden = (silu_gate * up_pre).astype(jnp.bfloat16)
-    expert_out = from_experts(
-        jnp.einsum("ecf,edf->ecd", hidden, down_full, preferred_element_type=jnp.float32).astype(
-            jnp.bfloat16
-        )
-    )
+    expert_rows = jnp.einsum(
+        "ecf,edf->ecd", hidden, down_full, preferred_element_type=jnp.float32
+    ).astype(jnp.bfloat16)
     grad_hidden = jnp.einsum(
         "ecd,edf->ecf", grad_expert, down_full, preferred_element_type=jnp.float32
     )
@@ -332,44 +331,43 @@
         "ecf,edf->ecd", grad_up_pre, up_full, preferred_element_type=jnp.float32
     )
     routed_slots = from_experts(grad_expert_in.astype(jnp.bfloat16))
-    grad_stack = jnp.stack(
-        [
-            jnp.einsum("ecd,ecf->edf", left, right, preferred_element_type=jnp.float32).astype(
-                jnp.bfloat16
-            )
-            for left, right in (
-                (expert_in, grad_gate_pre),
-                (expert_in, grad_up_pre),
-                (grad_expert, hidden),
-            )
-        ],
-        1,
+    grad_gate_w, grad_up_w, grad_down_w = (
+        jnp.einsum("ecd,ecf->edf", left, right, preferred_element_type=jnp.float32).astype(
+            jnp.bfloat16
+        )
+        for left, right in (
+            (expert_in, grad_gate_pre),
+            (expert_in, grad_up_pre),
+            (grad_expert, hidden),
+        )
     )
     if owns_experts:
-        grad_shards = lax.all_to_all(
-            grad_stack.reshape(3, local_experts, rows_shard, -1).transpose(1, 0, 2, 3),
+        grad_gate_w, grad_up_w, grad_down_w = (
+            value.reshape(local_experts, rows_shard, width)
+            for value in (grad_gate_w, grad_up_w, grad_down_w)
+        )
+        moved = lax.all_to_all(
+            jnp.concatenate(
+                [
+                    jnp.concatenate([grad_gate_w, grad_up_w], 2),
+                    jnp.concatenate([grad_down_w[:, :half], grad_down_w[:, half:]], 2),
+                    expert_rows.reshape(local_experts, capacity, D),
+                ],
+                1,
+            ),
             "dp",
             split_axis=0,
             concat_axis=0,
             tiled=True,
         )
     else:
-        grad_shards = lax.psum_scatter(grad_stack, "dp", scatter_dimension=2, tiled=True)
-    grad_shards = grad_shards.astype(jnp.float32)
-    grad_gate, grad_up = (grad_shards[:, 0], grad_shards[:, 1])
-    grad_down = grad_shards[:, 2].transpose(0, 2, 1)
-
+        grad_gate, grad_up, grad_down = (
+            lax.psum_scatter(value, "dp", scatter_dimension=1, tiled=True).astype(jnp.float32)
+            for value in (grad_gate_w, grad_up_w, grad_down_w)
+        )
+        expert_out = expert_rows.reshape(-1, D)
     routed_part = jnp.dot(slot_rows, routed_slots, preferred_element_type=jnp.float32)
     grad_routed = sum_rows(routed_part)
-    combined = jnp.dot(gated_rows, expert_out, preferred_element_type=jnp.float32)
-    layer_out = (attended + sum_rows(combined)).astype(jnp.bfloat16)
-    gate_grad = jnp.sum(grad_slots * expert_out.astype(jnp.float32), -1)
-    row_grads = jnp.sum(
-        jnp.where(slots, gate_grad.reshape(1, local_experts, capacity), 0.0), -1
-    )
-    gate_part = jnp.sum(jnp.where(pairs, row_grads[:, None, :], 0.0), -1)
-    grad_gates = lax.psum_scatter(gate_part, "tensor", scatter_dimension=0, tiled=True)
-
     gain_ffn_part, attended_norm = normalize_back(grad_routed, scaled_ffn, factor_ffn, gain_ffn)
     grad_attended = cotangent.astype(jnp.float32) + attended_norm
     grad_branch = spread(grad_attended.astype(jnp.bfloat16))
@@ -387,17 +385,29 @@
         rotate_back(grad_keys, cosine, sine_table).astype(jnp.bfloat16).reshape(group_rows, -1)
     )
     grad_pre = jnp.concatenate([grad_query_pre, grad_key_pre, grad_values.astype(jnp.bfloat16)], 1)
+    if owns_experts:
+        moved, grad_pre = lax.optimization_barrier((moved, grad_pre))
+        grad_gate = moved[:, :rows_shard, :width].astype(jnp.float32)
+        grad_up = moved[:, :rows_shard, width:].astype(jnp.float32)
+        down_moved = moved[:, rows_shard : rows_shard + half].astype(jnp.float32)
+        grad_down = jnp.concatenate([down_moved[:, :, :width], down_moved[:, :, width:]], 1)
+        expert_out = moved[:, rows_shard + half :].reshape(-1, D)
+    grad_down = grad_down.transpose(0, 2, 1)
+    combined = jnp.dot(gated_rows, expert_out, preferred_element_type=jnp.float32)
+    layer_out = (attended + sum_rows(combined)).astype(jnp.bfloat16)
+    gate_grad = jnp.sum(grad_slots * expert_out.astype(jnp.float32), -1)
+    row_grads = jnp.sum(
+        jnp.where(slots, gate_grad.reshape(1, local_experts, capacity), 0.0), -1
+    )
+    gate_part = jnp.sum(jnp.where(pairs, row_grads[:, None, :], 0.0), -1)
+    grad_gates = lax.psum_scatter(gate_part, "tensor", scatter_dimension=0, tiled=True)
     grad_pre_w = jnp.einsum("td,tc->dc", normed, grad_pre, preferred_element_type=jnp.float32)
     grad_normed = sum_rows(
         jnp.einsum("tc,dc->td", grad_pre, pre_full, preferred_element_type=jnp.float32)
     )
     gain_attn_part, tokens_norm = normalize_back(grad_normed, scaled_attn, factor_attn, gain_attn)
     grad_tokens = grad_attended + tokens_norm
-    gain_parts = lax.all_gather(
-        jnp.stack([gain_attn_part, gain_ffn_part]), ("dp", "tensor"), axis=0, tiled=False
-    )
-    gain_sums = jnp.sum(gain_parts, 0)
-    grad_gain_attn, grad_gain_ffn = (gain_sums[0], gain_sums[1])
+    grad_gain_attn, grad_gain_ffn = lax.psum((gain_attn_part, gain_ffn_part), ("dp", "tensor"))
     attn_moved = lax.all_to_all(
         jnp.concatenate(
             [grad_pre_w.astype(jnp.bfloat16), grad_out_w.astype(jnp.bfloat16)], 1

time: 909 us -> 888 us (0.977)
  blocking collectives: 89.5 us -> 41.9 us
  waiting for transfers between devices: 518 us -> 479 us
  starting transfers between devices: 102 us -> 132 us
  other arithmetic: 44.7 us -> 63 us
  local copies, waits for them, and re-layouts: 31.7 us -> 49.8 us
    all_to_all x2 -> x1, waiting for transfers between devices: 166 us -> 71.6 us  [from_experts(): lax.all_to_all(rows.reshape(local_experts, capacity, D), 'dp', split_axis...]
    all_gather x1 -> x0, blocking collectives: 89.5 us -> none  [on_device(): lax.all_gather(jnp.stack([gain_attn_part, gain_ffn_part]), ('dp', 'tensor...]
    all_to_all x1, waiting for transfers between devices: 0.01 us -> 86.4 us  [on_device(): lax.all_to_all(jnp.concatenate([jnp.concatenate([w_gate, w_up], 2), jnp.c...]
    all_gather x1, waiting for transfers between devices: 122 us -> 48.1 us  [on_device(): lax.all_gather(jnp.concatenate([w_query, w_key, w_value, w_out.T], 1), 'd...]
    all_to_all x1, waiting for transfers between devices: 32.1 us -> 88.2 us  [on_device(): lax.all_to_all(jnp.concatenate([jnp.concatenate([grad_gate_w, grad_up_w],...]
    psum x0 -> x1, blocking collectives: none -> 41.9 us  [on_device(): lax.psum((gain_attn_part, gain_ffn_part), ('dp', 'tensor'))]
    all_to_all x1, starting transfers between devices: 5.65 us -> 36.5 us  [to_experts(): lax.all_to_all(rows.reshape(local_experts, capacity, D), 'dp', split_axis...]
    all_to_all x2 -> x1, starting transfers between devices: 47.8 us -> 24.1 us  [from_experts(): lax.all_to_all(rows.reshape(local_experts, capacity, D), 'dp', split_axis...]
  transfers between devices with their start and end apart: 16 -> 15, of which waited for: 12 -> 11; matrix products, arithmetic and copies ran while one was open for 15% -> 18% of each run, Pallas kernels for 0% -> 0%
where the time goes in v3:
time: 888 us; the launch traced here: 882 us
  waiting for transfers between devices  479 us (54%)
  starting transfers between devices  132 us (15%)
  matrix products  101 us (11%)
  other arithmetic  63 us (7%)
  local copies, waits for them, and re-layouts  49.8 us (6%)
  blocking collectives  41.9 us (5%)
  between operations  15.6 us (2%)
    all_to_all x1, waiting for transfers between devices, on_device(): lax.all_to_all(jnp.concatenate([jnp.concatenate([grad_gate_w, grad_up_w],...  88.2 us
    all_to_all x1, waiting for transfers between devices, on_device(): lax.all_to_all(jnp.concatenate([jnp.concatenate([w_gate, w_up], 2), jnp.c...  86.4 us
    all_to_all x1, waiting for transfers between devices, to_experts(): lax.all_to_all(rows.reshape(local_experts, capacity, D), 'dp', split_axis...  82.7 us
    all_gather x4, waiting for transfers between devices, spread(): return lax.all_gather(values, 'tensor', axis=0, tiled=True)  76.4 us
    all_to_all x1, waiting for transfers between devices, from_experts(): lax.all_to_all(rows.reshape(local_experts, capacity, D), 'dp', split_axis...  71.6 us
    all_gather x1, waiting for transfers between devices, on_device(): lax.all_gather(jnp.concatenate([w_query, w_key, w_value, w_out.T], 1), 'd...  48.1 us
    psum x1, blocking collectives, on_device(): lax.psum((gain_attn_part, gain_ffn_part), ('dp', 'tensor'))  41.9 us
    all_to_all x1, starting transfers between devices, on_device(): lax.all_to_all(jnp.concatenate([grad_pre_w.astype(jnp.bfloat16), grad_out...  36.5 us
  transfers between devices with their start and end apart: 15, of which 11 were waited for; matrix products, arithmetic and copies ran while one was open for 18% of the time, Pallas kernels for 0%

profile of v3, /device:TPU:0, one launch (start us, length us, event | category | flops | bytes accessed | tf_op | source)
XLA Modules:
  0.0 882.0 jit_solution(8499821974822052201)
XLA Ops:
  9.8 2.0 fusion.24
  11.9 1.6 pad_maximum_fusion.6
  17.2 16.4 %all-gather.10.cloned.1.call-done = bf16[512,1024]{1,0:T(8,128)(2,1)} async-done(((bf16[256,1024]{1,0:T(8,128)(2,1)}), bf16[512,1024]{1,0:T(8,128)(2,1)}) %all-gather.10.cloned.1.call-update) | async-done | bytes 1048592 | tf_op jit(solution)/shard_map/all_gather | solution.py:59
  33.6 8.5 multiply_convert_fusion
  42.1 15.0 %all-gather.8.cloned.1.call-done = bf16[512,1024]{1,0:T(8,128)(2,1)} async-done(((bf16[256,1024]{1,0:T(8,128)(2,1)}), bf16[512,1024]{1,0:T(8,128)(2,1)}) %all-gather.8.cloned.1.call-update) | async-done | bytes 1048592 | tf_op jit(solution)/shard_map/all_gather | solution.py:59
  57.1 48.1 %all-gather.6.cloned.1.call-done = bf16[1024,1536]{1,0:T(8,128)(2,1)} async-done(((bf16[64,1536]{1,0:T(8,128)(2,1)}), bf16[1024,1536]{1,0:T(8,128)(2,1)}) %all-gather.6.cloned.1.call-update) | async-done | bytes 3145744 | tf_op jit(solution)/shard_map/all_gather | solution.py:219
  105.2 8.1 copy.74
  113.3 6.3 pad_maximum_fusion
  119.6 4.9 all-to-all-start.1
  125.3 2.9 fusion.14
  134.6 1.8 exponential_reduce_fusion
  136.4 2.3 convolution_convert_fusion.7
  138.7 2.2 fusion.36
  142.3 1.5 collective-permute-start
  143.9 12.6 %collective-permute-done = bf16[256,1024]{1,0:T(8,128)(2,1)S(1)} collective-permute-done((bf16[256,1024]{1,0:T(8,128)(2,1)S(1)}, bf16[256,1024]{1,0:T(8,128)(2,1)S(1)}, u32[]{:S(2)}, u32[]{:S(2)}) %collective-permute-start) | collective-permute-done | bytes 524320 | tf_op jit(solution)/shard_map/ppermute | solution.py:70
  156.5 1.5 multiply_reduce_fusion.3
  159.0 22.6 %all-gather.12.cloned.1.call-done = bf16[512,1024]{1,0:T(8,128)(2,1)} async-done(((bf16[256,1024]{1,0:T(8,128)(2,1)}), bf16[512,1024]{1,0:T(8,128)(2,1)}) %all-gather.12.cloned.1.call-update) | async-done | bytes 1048592 | tf_op jit(solution)/shard_map/all_gather | solution.py:59
  181.6 7.2 convolution_convert_fusion
  188.8 86.4 %all-to-all-done.1 = bf16[16,256,1024]{2,1,0:T(8,128)(2,1)} async-done(((bf16[16,256,1024]{2,1,0:T(8,128)(2,1)}), bf16[16,256,1024]{2,1,0:T(8,128)(2,1)}, u32[]{:S(2)}, u32[]{:S(2)}) %all-to-all-start.1) | async-done | bytes 8388640 | tf_op jit(solution)/shard_map/all_to_all | solution.py:259
  275.1 36.5 %all-to-all-start = ((bf16[16,160,1024]{2,1,0:T(8,128)(2,1)}), bf16[16,160,1024]{2,1,0:T(8,128)(2,1)}, u32[]{:S(2)}, u32[]{:S(2)}) async-start(bf16[16,160,1024]{2,1,0:T(8,128)(2,1)} %bitcast.152), calls=%async_computation | async-start | bytes 10485760 | tf_op jit(solution)/shard_map/all_to_all | solution.py:225
  311.7 3.4 slice.141
  315.1 2.1 fusion.53
  317.3 3.1 fusion.54
  320.4 4.5 fusion.61
  324.9 82.7 %all-to-all-done = bf16[16,160,1024]{2,1,0:T(8,128)(2,1)} async-done(((bf16[16,160,1024]{2,1,0:T(8,128)(2,1)}), bf16[16,160,1024]{2,1,0:T(8,128)(2,1)}, u32[]{:S(2)}, u32[]{:S(2)}) %all-to-all-start) | async-done | bytes 5242912 | tf_op jit(solution)/shard_map/all_to_all | solution.py:225
  407.6 5.2 fusion.62
  412.9 8.7 multiply_convert_fusion.3
  421.6 2.9 fusion.63
  424.5 5.1 add_convert_fusion
  429.6 24.1 %all-to-all-start.3 = ((bf16[16,160,1024]{2,1,0:T(8,128)(2,1)}), bf16[16,160,1024]{2,1,0:T(8,128)(2,1)}, u32[]{:S(2)}, u32[]{:S(2)}) async-start(bf16[16,160,1024]{2,1,0:T(8,128)(2,1)} %bitcast.151), calls=%async_computation.3 | async-start | bytes 10485760 | tf_op jit(solution)/shard_map/all_to_all | solution.py:233
  453.7 6.3 convolution_convert_fusion.3
  460.2 3.2 convolution_convert_fusion.1
  463.4 5.6 convolution_convert_fusion.5
  468.9 5.4 convolution_convert_fusion.4
  474.3 3.7 pad_maximum_fusion.1
  478.1 71.6 %all-to-all-done.3 = bf16[16,160,1024]{2,1,0:T(8,128)(2,1)} async-done(((bf16[16,160,1024]{2,1,0:T(8,128)(2,1)}), bf16[16,160,1024]{2,1,0:T(8,128)(2,1)}, u32[]{:S(2)}, u32[]{:S(2)}) %all-to-all-start.3) | async-done | bytes 5242912 | tf_op jit(solution)/shard_map/all_to_all | solution.py:233
  549.6 23.9 %all-to-all-start.2 = ((bf16[16,256,1024]{2,1,0:T(8,128)(2,1)}), bf16[16,256,1024]{2,1,0:T(8,128)(2,1)}, u32[]{:S(2)}, u32[]{:S(2)}) async-start(bf16[16,256,1024]{2,1,0:T(8,128)(2,1)} %pad_maximum_fusion.1), calls=%async_computation.2 | async-start | bytes 16777216 | tf_op jit(solution)/shard_map/all_to_all | solution.py:349
  573.9 5.0 fusion.17
  578.9 1.5 collective-permute-start.1
  580.5 12.7 %collective-permute-done.1 = bf16[256,1024]{1,0:T(8,128)(2,1)S(1)} collective-permute-done((bf16[256,1024]{1,0:T(8,128)(2,1)S(1)}, bf16[256,1024]{1,0:T(8,128)(2,1)S(1)}, u32[]{:S(2)}, u32[]{:S(2)}) %collective-permute-start.1) | collective-permute-done | bytes 524320 | tf_op jit(solution)/shard_map/ppermute | solution.py:70
  595.4 22.5 %all-gather.14.cloned.1.call-done = bf16[512,1024]{1,0:T(8,128)(2,1)} async-done(((bf16[256,1024]{1,0:T(8,128)(2,1)}), bf16[512,1024]{1,0:T(8,128)(2,1)}) %all-gather.14.cloned.1.call-update) | async-done | bytes 1048592 | tf_op jit(solution)/shard_map/all_gather | solution.py:59
  617.9 2.3 convolution_convert_fusion.8
  620.2 5.1 fusion
  626.2 2.7 fusion.2
  632.0 2.2 fusion.22
  634.3 1.7 convolution_convert_fusion.6
  636.0 88.2 %all-to-all-done.2 = bf16[16,256,1024]{2,1,0:T(8,128)(2,1)} async-done(((bf16[16,256,1024]{2,1,0:T(8,128)(2,1)}), bf16[16,256,1024]{2,1,0:T(8,128)(2,1)}, u32[]{:S(2)}, u32[]{:S(2)}) %all-to-all-start.2) | async-done | bytes 8388640 | tf_op jit(solution)/shard_map/all_to_all | solution.py:349
  724.2 2.6 convolution_convert_fusion.2
  726.8 1.9 pad_maximum_fusion.2
  728.8 4.7 copy.79
  733.4 36.5 %all-to-all-start.4 = ((bf16[16,64,1536]{2,1,0:T(8,128)(2,1)}), bf16[16,64,1536]{2,1,0:T(8,128)(2,1)}, u32[]{:S(2)}, u32[]{:S(2)}) async-start(bf16[16,64,1536]{2,1,0:T(8,128)(2,1)} %bitcast.146), calls=%async_computation.5 | async-start | bytes 6291456 | tf_op jit(solution)/shard_map/all_to_all | solution.py:411
  770.0 2.9 fusion.12
  775.9 3.4 slice.122
  779.4 4.9 fusion.16
  787.1 5.6 bitcast_convert_fusion
  792.7 11.5 %copy.78 = f32[2560,1024]{0,1:T(8,128)} copy(f32[2560,1024]{1,0:T(8,128)} %bitcast_convert_fusion) | data formatting | bytes 20971520 | tf_op jit(solution)/shard_map/convert_element_type | solution.py:398
  804.2 8.1 multiply_reduce_fusion
  812.4 1.5 select_reduce_fusion.1
  815.4 1.5 fusion.55
  817.8 4.3 slice_convert_fusion.1
  824.2 41.9 %all-reduce = (f32[1024]{0:T(1024)}, f32[1024]{0:T(1024)}) all-reduce(f32[1024]{0:T(1024)S(1)} %get-tuple-element.69, f32[1024]{0:T(1024)S(1)} %copy-done.37), channel_id=1, replica_groups=mesh['dp'=16,'tensor'=2] {'dp','tensor'}, use_global_device_ids=true, to_apply=%region_15.16 | all-reduce | flops 2048 | bytes 16384 | tf_op jit(solution)/shard_map/psum | solution.py:410
  866.0 2.4 add_convert_fusion.1
  868.5 2.5 fusion.28
  871.0 2.4 convert_reduce_fusion
  (182 shorter events, 33.9 us)
Async XLA Ops:
  7.2 9.9 %copy-start.19 = (bf16[16,512,64]{1,2,0:T(8,128)(2,1)S(1)}, bf16[16,512,64]{1,2,0:T(8,128)(2,1)}, u32[]{:S(2)}) copy-start(bf16[16,512,64]{1,2,0:T(8,128)(2,1)} %param.22) | copy-start | bytes 3145732
  7.2 26.4 %all-gather.10.cloned.1.call-start = ((), (), s32[]{:S(2)}) async-start(), calls=%async_computation.8 | async-start | bytes 1572864 | tf_op jit(solution)/shard_map/all_gather | solution.py:59
  7.9 49.1 %all-gather.8.cloned.1.call-start = ((), (), s32[]{:S(2)}) async-start(), calls=%async_computation.7 | async-start | bytes 1572864 | tf_op jit(solution)/shard_map/all_gather | solution.py:59
  11.8 93.3 %all-gather.6.cloned.1.call-start = ((), (), s32[]{:S(2)}) async-start(), calls=%async_computation.6 | async-start | bytes 3342336 | tf_op jit(solution)/shard_map/all_gather | solution.py:219
  13.6 1.7 copy-start.41
  15.3 1.8 copy-start.29
  15.6 1.5 copy-start.25
  17.1 25.0 %copy-start.4 = (pred[512,2560]{0,1:T(32,128)(4,1)}, pred[512,2560]{0,1:T(32,128)(4,1)S(1)}, u32[]{:S(2)}) copy-start(pred[512,2560]{0,1:T(32,128)(4,1)S(1)} %bitcast_compare_fusion) | copy-start | bytes 3932164
  105.2 8.1 copy-start.17
  105.2 8.1 copy-start.18
  119.6 5.7 copy-start.43
  119.6 155.6 %all-to-all-start.1 = ((bf16[16,256,1024]{2,1,0:T(8,128)(2,1)}), bf16[16,256,1024]{2,1,0:T(8,128)(2,1)}, u32[]{:S(2)}, u32[]{:S(2)}) async-start(bf16[16,256,1024]{2,1,0:T(8,128)(2,1)} %pad_maximum_fusion), calls=%async_computation.1 | async-start | bytes 16777216 | tf_op jit(solution)/shard_map/all_to_all | solution.py:259
  124.5 57.0 %all-gather.12.cloned.1.call-start = ((), (), s32[]{:S(2)}) async-start(), calls=%async_computation.9 | async-start | bytes 1572864 | tf_op jit(solution)/shard_map/all_gather | solution.py:59
  125.2 6.4 copy-start.10
  131.8 2.8 copy-start.12
  134.6 4.2 copy-start
  134.6 1.8 copy-start.15
  136.4 20.1 %copy-start.1 = (bf16[256,1024]{1,0:T(8,128)(2,1)S(1)}, bf16[256,1024]{1,0:T(8,128)(2,1)}, u32[]{:S(2)}) copy-start(bf16[256,1024]{1,0:T(8,128)(2,1)} %param.13) | copy-start | bytes 1572868
  138.7 3.6 copy-start.23
  138.7 19.3 %copy-start.32 = (f32[1024]{0:T(1024)S(1)}, f32[1024]{0:T(1024)}, u32[]{:S(2)}) copy-start(f32[1024]{0:T(1024)} %param.15) | copy-start | bytes 12292
  142.3 14.1 %collective-permute-start = (bf16[256,1024]{1,0:T(8,128)(2,1)S(1)}, bf16[256,1024]{1,0:T(8,128)(2,1)S(1)}, u32[]{:S(2)}, u32[]{:S(2)}) collective-permute-start(bf16[256,1024]{1,0:T(8,128)(2,1)S(1)} %dynamic-slice_convert_fusion.3), channel_id=1, source_target_pairs={{0,1},{1,0},{2,3},{3,2},{4,5},{5,4},{6,7},{7,6},{8,9},{9,8},{10,11... | collective-permute-start | bytes 1572872 | tf_op jit(solution)/shard_map/ppermute | solution.py:70
  158.0 30.8 %copy-start.38 = (f32[256]{0:T(256)}, f32[256]{0:T(256)S(1)}, u32[]{:S(2)}) copy-start(f32[256]{0:T(256)S(1)} %add_rsqrt_fusion) | copy-start | bytes 3076
  275.1 132.5 %all-to-all-start = ((bf16[16,160,1024]{2,1,0:T(8,128)(2,1)}), bf16[16,160,1024]{2,1,0:T(8,128)(2,1)}, u32[]{:S(2)}, u32[]{:S(2)}) async-start(bf16[16,160,1024]{2,1,0:T(8,128)(2,1)} %bitcast.152), calls=%async_computation | async-start | bytes 10485760 | tf_op jit(solution)/shard_map/all_to_all | solution.py:225
  315.1 5.3 copy-start.5
  407.6 5.2 copy-start.21
  407.6 5.3 copy-start.50
  421.6 2.9 copy-start.45
  421.6 2.9 copy-start.47
  421.6 3.0 copy-start.20
  429.6 120.0 %all-to-all-start.3 = ((bf16[16,160,1024]{2,1,0:T(8,128)(2,1)}), bf16[16,160,1024]{2,1,0:T(8,128)(2,1)}, u32[]{:S(2)}, u32[]{:S(2)}) async-start(bf16[16,160,1024]{2,1,0:T(8,128)(2,1)} %bitcast.151), calls=%async_computation.3 | async-start | bytes 10485760 | tf_op jit(solution)/shard_map/all_to_all | solution.py:233
  453.7 6.5 copy-start.49
  460.2 3.2 copy-start.46
  463.4 5.6 copy-start.48
  478.1 95.8 %copy-start.26 = (s32[512,16]{0,1:T(8,128)S(1)}, s32[512,16]{0,1:T(8,128)}, u32[]{:S(2)}) copy-start(s32[512,16]{0,1:T(8,128)} %copy-done.25) | copy-start | bytes 98308
  549.6 174.6 %all-to-all-start.2 = ((bf16[16,256,1024]{2,1,0:T(8,128)(2,1)}), bf16[16,256,1024]{2,1,0:T(8,128)(2,1)}, u32[]{:S(2)}, u32[]{:S(2)}) async-start(bf16[16,256,1024]{2,1,0:T(8,128)(2,1)} %pad_maximum_fusion.1), calls=%async_computation.2 | async-start | bytes 16777216 | tf_op jit(solution)/shard_map/all_to_all | solution.py:349
  573.5 19.6 %copy-start.33 = (f32[1024]{0:T(1024)S(1)}, f32[1024]{0:T(1024)}, u32[]{:S(2)}) copy-start(f32[1024]{0:T(1024)} %param.15) | copy-start | bytes 12292
  573.5 19.6 %copy-start.39 = (f32[256]{0:T(256)S(1)}, f32[256]{0:T(256)}, u32[]{:S(2)}) copy-start(f32[256]{0:T(256)} %copy-done.38) | copy-start | bytes 3076
  573.6 44.3 %all-gather.14.cloned.1.call-start = ((), (), s32[]{:S(2)}) async-start(), calls=%async_computation.10 | async-start | bytes 1572864 | tf_op jit(solution)/shard_map/all_gather | solution.py:59
  573.8 20.3 %copy-start.14 = (bf16[256,1024]{1,0:T(8,128)(2,1)S(1)}, bf16[256,1024]{1,0:T(8,128)(2,1)}, u32[]{:S(2)}) copy-start(bf16[256,1024]{1,0:T(8,128)(2,1)} %param.25) | copy-start | bytes 1572868
  573.8 20.3 %copy-start.34 = (f32[1024]{0:T(1024)S(1)}, f32[1024]{0:T(1024)}, u32[]{:S(2)}) copy-start(f32[1024]{0:T(1024)} %param.15) | copy-start | bytes 12292
  573.9 20.3 %copy-start.40 = (f32[256]{0:T(256)S(1)}, f32[256]{0:T(256)}, u32[]{:S(2)}) copy-start(f32[256]{0:T(256)} %copy-done.38) | copy-start | bytes 3076
  578.9 14.2 %collective-permute-start.1 = (bf16[256,1024]{1,0:T(8,128)(2,1)S(1)}, bf16[256,1024]{1,0:T(8,128)(2,1)S(1)}, u32[]{:S(2)}, u32[]{:S(2)}) collective-permute-start(bf16[256,1024]{1,0:T(8,128)(2,1)S(1)} %dynamic-slice_convert_fusion.2), channel_id=1, source_target_pairs={{0,1},{1,0},{2,3},{3,2},{4,5},{5,4},{6,7},{7,6},{8,9},{9,8},{10,11... | collective-permute-start | bytes 1572872 | tf_op jit(solution)/shard_map/ppermute | solution.py:70
  620.2 5.2 slice-start
  620.2 6.0 slice-start.1
  626.2 2.7 copy-start.13
  631.9 2.3 copy-start.24
  632.0 2.3 copy-start.44
  724.2 2.6 copy-start.22
  733.4 137.6 %all-to-all-start.4 = ((bf16[16,64,1536]{2,1,0:T(8,128)(2,1)}), bf16[16,64,1536]{2,1,0:T(8,128)(2,1)}, u32[]{:S(2)}, u32[]{:S(2)}) async-start(bf16[16,64,1536]{2,1,0:T(8,128)(2,1)} %bitcast.146), calls=%async_computation.5 | async-start | bytes 6291456 | tf_op jit(solution)/shard_map/all_to_all | solution.py:411
  769.9 104.8 %reduce-scatter.2.cloned.1.call-start = ((), (), s32[]{:S(2)}) async-start(), calls=%async_computation.11 | async-start | bytes 24576 | tf_op jit(solution)/shard_map/reduce_scatter | solution.py:403
  772.9 1.6 copy-start.8
  774.5 4.9 copy-start.27
  774.5 4.9 copy-start.30
  774.5 49.2 %collective-permute-start.3 = (bf16[256,1024]{1,0:T(8,128)(2,1)}, bf16[256,1024]{1,0:T(8,128)(2,1)S(1)}, u32[]{:S(2)}, u32[]{:S(2)}) collective-permute-start(bf16[256,1024]{1,0:T(8,128)(2,1)} %dynamic-slice_convert_fusion), channel_id=1, source_target_pairs={{0,1},{1,0},{2,3},{3,2},{4,5},{5,4},{6,7},{7,6},{8,9},{9,8},{10,11... | collective-permute-start | bytes 1572872 | tf_op jit(solution)/shard_map/ppermute | solution.py:70
  786.5 79.5 %collective-permute-start.2 = (bf16[256,1024]{1,0:T(8,128)(2,1)}, bf16[256,1024]{1,0:T(8,128)(2,1)}, u32[]{:S(2)}, u32[]{:S(2)}) collective-permute-start(bf16[256,1024]{1,0:T(8,128)(2,1)} %dynamic-slice_convert_fusion.1), channel_id=1, source_target_pairs={{0,1},{1,0},{2,3},{3,2},{4,5},{5,4},{6,7},{7,6},{8,9},{9,8},{10,11... | collective-permute-start | bytes 1572872 | tf_op jit(solution)/shard_map/ppermute | solution.py:70
  812.3 4.7 copy-start.28
  812.3 4.7 copy-start.42
  817.7 4.4 copy-start.6
  817.8 4.4 copy-start.7
  817.8 5.9 copy-start.2
  817.8 5.8 copy-start.9
  817.8 5.8 copy-start.31
  817.8 5.8 copy-start.36
  817.8 6.3 copy-start.37
  (4 other events, 4.5 us)
Sparse Core Ops, SparseCore 0:
  9.6 24.0 all-gather.9
  35.7 21.2 all-gather.7
  59.9 45.1 all-gather.5
  159.1 22.4 all-gather.11
  595.5 22.3 all-gather.13
  817.9 10.9 reduce-scatter.1
